TPU v7x, 32 devices: a whole 2x2x4 slice. The times are simulated.
32 devices in a mesh: ctx: 8 (over z, core), head: 4 (over y, x).
Axes of the slice: x: 2, y: 2, z: 4, core: 2. Of those that a mesh axis runs over, the one named last changes fastest.
Arguments:
- attn_q: bfloat16 [1024, 4096], P('ctx', 'head'), may hold values from -6 to 6
- attn_k: bfloat16 [1024, 512], P('ctx'), may hold values from -6 to 6
- attn_v: bfloat16 [1024, 512], P('ctx'), may hold values from -0.375 to 0.375
- attn_cot: bfloat16 [1024, 4096], P('ctx', 'head'), may hold values from -6 to 6
- attn_lse: float32 [16, 1024], P('head'), may hold values from 3 to 6
- attn_delta: float32 [16, 1024], P('head'), may hold values from -6 to 6
- block_lists: int32 [16, 16, 4], P('head'), may hold values from 0 to 15, as said below
- gdn_q: bfloat16 [1024, 2048], P('ctx', 'head'), may hold values from -6 to 6
- gdn_k: bfloat16 [1024, 2048], P('ctx', 'head'), may hold values from -6 to 6
- gdn_v: bfloat16 [1024, 4096], P('ctx', 'head'), may hold values from -6 to 6
- decay_logit: float32 [32, 1024], P('head', 'ctx'), may hold values from -8 to 8
- write_logit: float32 [32, 1024], P('head', 'ctx'), may hold values from -6 to 6
- decay_rate: float32 [32], P('head'), may hold values from 0.0009765625 to 0.1
- write_scale: float32 [32], P('head'), may hold values from 0.05 to 1
- gdn_cot: bfloat16 [1024, 4096], P('ctx', 'head'), may hold values from -6 to 6
Outputs:
- attn_dq: float32 [1024, 4096], P('ctx', 'head')
- attn_dk: float32 [1024, 512], P('ctx')
- attn_dv: float32 [1024, 512], P('ctx')
- gdn_dq: float32 [1024, 2048], P('ctx', 'head')
- gdn_dk: float32 [1024, 2048], P('ctx', 'head')
- gdn_dv: float32 [1024, 4096], P('ctx', 'head')
- gdn_ddecay: float32 [32, 1024], P('head', 'ctx')
- gdn_dwrite: float32 [32, 1024], P('head', 'ctx')
Inputs may be any that keep to these rules, and one draw needn't show every extreme that they name: `block_lists`: entries for query block b lie in 0 to b and may repeat.
All inputs are finite; a program needn't handle non-finite values.
Results may differ from a plain program's by a relative error of at most 0.00035.
Values may be sent and summed in bfloat16 or wider, within the bound.
A program may use at most 128 MiB of HBM per device.

v0:
```python
import jax
import jax.numpy as jnp
from jax import lax
from jax.sharding import PartitionSpec as P

Q_HEADS = 16
KV_HEADS = 2
HD = 256
GDIM = 128
BLK = 64
TOPK = 4
SPAN = 64


HIGHEST = lax.Precision.HIGHEST


def prefix(value, axis, join, neutral, backward):
    count, mine = (lax.axis_size(axis), lax.axis_index(axis))
    pieces = jax.tree.map(lambda part: lax.all_gather(part, axis), value)
    if backward:
        pieces = jax.tree.map(lambda part: part[::-1], pieces)
        mine = count - 1 - mine
    so_far = jax.tree.map(
        lambda part, zero: jnp.full_like(part, 0) + jnp.asarray(zero, part.dtype), value, neutral
    )

    def turn(position, so_far):
        longer = join(so_far, jax.tree.map(lambda part: part[position], pieces))
        return jax.tree.map(lambda new, old: jnp.where(position < mine, new, old), longer, so_far)

    return lax.fori_loop(0, count - 1, turn, so_far)


def unit_rows(matrix):
    return matrix / jnp.sqrt(jnp.sum(matrix * matrix, axis=-1, keepdims=True) + 1e-06)


def span_update(memory, packed):
    queries, keys_in, values_in, log_decay, write_gain = packed
    length = log_decay.shape[-1]
    cum_log = jnp.cumsum(log_decay, axis=-1)
    log_gap = cum_log[:, :, None] - cum_log[:, None, :]
    order_ids = jnp.arange(length)
    strict_low = order_ids[:, None] > order_ids[None, :]
    with_diag = order_ids[:, None] >= order_ids[None, :]
    decay_strict = jnp.where(strict_low, jnp.exp(jnp.where(strict_low, log_gap, 0.0)), 0.0)
    decay_upto = jnp.where(with_diag, jnp.exp(jnp.where(with_diag, log_gap, 0.0)), 0.0)
    key_gram = jnp.einsum("htd,hsd->hts", keys_in, keys_in, precision=HIGHEST)
    system = write_gain[:, :, None] * decay_strict * key_gram + jnp.eye(length, dtype=jnp.float32)
    decay_now = jnp.exp(cum_log)
    recalled = jnp.einsum("hvd,htd->htv", memory, keys_in, precision=HIGHEST)
    target = write_gain[:, :, None] * (values_in - decay_now[:, :, None] * recalled)
    written = lax.linalg.triangular_solve(
        system, target, left_side=True, lower=True, unit_diagonal=True
    )
    read_old = jnp.einsum("hvd,htd->htv", memory, queries, precision=HIGHEST)
    query_key = jnp.einsum("htd,hsd->hts", queries, keys_in, precision=HIGHEST)
    outputs = decay_now[:, :, None] * read_old + jnp.einsum(
        "hts,hsv->htv", decay_upto * query_key, written, precision=HIGHEST
    )
    tail_decay = jnp.exp(cum_log[:, -1:] - cum_log)
    memory_next = jnp.exp(cum_log[:, -1])[:, None, None] * memory + jnp.einsum(
        "hsv,hsd->hvd", written * tail_decay[:, :, None], keys_in, precision=HIGHEST
    )
    return (memory_next, outputs)


def delta_forward(raw_inputs, memory, rate_heads, scale_heads):
    query_raw, key_raw, value_raw, decay_in, write_in = raw_inputs
    n_tokens = query_raw.shape[0]
    key_heads = query_raw.shape[1] // GDIM
    value_heads = value_raw.shape[1] // GDIM
    ratio_heads = value_heads // key_heads
    n_spans = n_tokens // SPAN
    queries = jnp.repeat(
        unit_rows(query_raw.reshape(n_tokens, key_heads, GDIM)), ratio_heads, axis=1
    )
    keys_norm = jnp.repeat(
        unit_rows(key_raw.reshape(n_tokens, key_heads, GDIM)), ratio_heads, axis=1
    )
    values_in = value_raw.reshape(n_tokens, value_heads, GDIM)
    log_decay = -rate_heads[:, None] * jax.nn.softplus(decay_in)
    write_gain = scale_heads[:, None] * jax.nn.sigmoid(write_in)

    def blocks_of(tensor):
        return tensor.reshape(n_spans, SPAN, value_heads, GDIM).transpose(0, 2, 1, 3)

    def gates_of(tensor):
        return tensor.reshape(value_heads, n_spans, SPAN).transpose(1, 0, 2)

    memory_end, outputs = lax.scan(
        span_update,
        memory,
        (
            blocks_of(queries),
            blocks_of(keys_norm),
            blocks_of(values_in),
            gates_of(log_decay),
            gates_of(write_gain),
        ),
    )
    return (outputs.transpose(0, 2, 1, 3).reshape(n_tokens, value_heads * GDIM), memory_end)


def sparse_query_grad(
    q_blocks,
    cot_blocks,
    own_keys,
    own_values,
    listed_keys,
    listed_values,
    lse_rows,
    delta_rows,
    head_lists,
    block_ids,
):
    score_scale = HD ** (-0.5)
    position = jnp.arange(BLK)
    causal = position[:, None] >= position[None, :]
    slot_ids = jnp.arange(TOPK)
    repeated = jnp.any(
        (head_lists[:, :, None] == head_lists[:, None, :])
        & (slot_ids[:, None] > slot_ids[None, :]),
        axis=2,
    )
    usable = (head_lists < block_ids[:, None]) & jnp.logical_not(repeated)
    own_score = (
        jnp.einsum("bid,bjd->bij", q_blocks, own_keys, preferred_element_type=jnp.float32)
        * score_scale
    )
    list_score = (
        jnp.einsum("bid,btjd->bitj", q_blocks, listed_keys, preferred_element_type=jnp.float32)
        * score_scale
    )
    own_prob = jnp.where(causal[None], jnp.exp(own_score - lse_rows[:, :, None]), 0.0)
    list_prob = jnp.where(
        usable[:, None, :, None], jnp.exp(list_score - lse_rows[:, :, None, None]), 0.0
    )
    own_dprob = jnp.einsum(
        "bid,bjd->bij", cot_blocks, own_values, preferred_element_type=jnp.float32
    )
    list_dprob = jnp.einsum(
        "bid,btjd->bitj", cot_blocks, listed_values, preferred_element_type=jnp.float32
    )
    own_dscore = own_prob * (own_dprob - delta_rows[:, :, None])
    list_dscore = list_prob * (list_dprob - delta_rows[:, :, None, None])
    own_part = jnp.einsum(
        "bij,bjd->bid", own_dscore, own_keys.astype(jnp.float32), precision=HIGHEST
    )
    list_part = jnp.einsum(
        "bitj,btjd->bid", list_dscore, listed_keys.astype(jnp.float32), precision=HIGHEST
    )
    return (own_part + list_part) * score_scale


def compose_maps(earlier, later):
    product = jnp.einsum("hij,hjk->hik", earlier[0], later[0], precision=HIGHEST)
    shifted = jnp.einsum("hij,hjk->hik", earlier[1], later[0], precision=HIGHEST) + later[1]
    return (product, shifted)


def on_device(
    attn_q,
    attn_k,
    attn_v,
    attn_cot,
    attn_lse,
    attn_delta,
    block_lists,
    gdn_q,
    gdn_k,
    gdn_v,
    decay_logit,
    write_logit,
    decay_rate,
    write_scale,
    gdn_cot,
):
    score_scale = HD ** (-0.5)
    head_index = lax.axis_index("head")
    ctx_index = lax.axis_index("ctx")
    tok_rows = attn_q.shape[0]
    local_heads = attn_q.shape[1] // HD
    blocks_here = tok_rows // BLK
    kv_group = head_index * local_heads // (Q_HEADS // KV_HEADS)
    own_keys = lax.dynamic_index_in_dim(
        attn_k.reshape(tok_rows, KV_HEADS, HD), kv_group, 1, keepdims=False
    )
    own_values = lax.dynamic_index_in_dim(
        attn_v.reshape(tok_rows, KV_HEADS, HD), kv_group, 1, keepdims=False
    )
    row_base = ctx_index * tok_rows
    first_block = ctx_index * blocks_here
    key_block_ids = first_block + jnp.arange(blocks_here, dtype=jnp.int32)
    member = jnp.any(block_lists[:, :, :, None] == key_block_ids[None, None, None, :], axis=2)
    member_rows = jnp.repeat(jnp.repeat(member, BLK, axis=1), BLK, axis=2)
    key_pos = row_base + jnp.arange(tok_rows, dtype=jnp.int32)
    key_block = key_pos // BLK
    keys_whole, values_whole = (
        lax.all_gather(own_keys, "ctx", axis=0, tiled=True),
        lax.all_gather(own_values, "ctx", axis=0, tiled=True),
    )
    lists_own = lax.dynamic_slice_in_dim(block_lists, first_block, blocks_here, 1)
    lse_own = lax.dynamic_slice_in_dim(attn_lse, row_base, tok_rows, 1).reshape(
        local_heads, blocks_here, BLK
    )
    delta_own = lax.dynamic_slice_in_dim(attn_delta, row_base, tok_rows, 1).reshape(
        local_heads, blocks_here, BLK
    )
    q_blocks = attn_q.reshape(blocks_here, BLK, local_heads, HD).transpose(2, 0, 1, 3)
    cot_blocks = attn_cot.reshape(blocks_here, BLK, local_heads, HD).transpose(2, 0, 1, 3)
    listed_keys = keys_whole.reshape(-1, BLK, HD)[lists_own]
    listed_values = values_whole.reshape(-1, BLK, HD)[lists_own]
    grad_blocks = jax.vmap(sparse_query_grad, in_axes=(0, 0, None, None, 0, 0, 0, 0, 0, None))(
        q_blocks,
        cot_blocks,
        own_keys.reshape(blocks_here, BLK, HD),
        own_values.reshape(blocks_here, BLK, HD),
        listed_keys,
        listed_values,
        lse_own,
        delta_own,
        lists_own,
        key_block_ids,
    )
    grad_q = grad_blocks.transpose(1, 2, 0, 3).reshape(tok_rows, local_heads * HD)
    query_rows = lax.all_gather(attn_q, "ctx", axis=0, tiled=True)
    n_rows = query_rows.shape[0]
    queries = query_rows.reshape(n_rows, local_heads, HD)
    cotangent = lax.all_gather(attn_cot, "ctx", axis=0, tiled=True).reshape(n_rows, local_heads, HD)
    row_pos = jnp.arange(n_rows, dtype=jnp.int32)
    row_block = row_pos // BLK
    own_pair = (row_block[:, None] == key_block[None, :]) & (row_pos[:, None] >= key_pos[None, :])
    listed_pair = member_rows & (key_block[None, :] < row_block[:, None])[None]
    allowed = own_pair[None] | listed_pair
    scores = (
        jnp.einsum("nhd,kd->hnk", queries, own_keys, preferred_element_type=jnp.float32)
        * score_scale
    )
    prob_full = jnp.where(allowed, jnp.exp(scores - attn_lse[:, :, None]), 0.0)
    dprobs = jnp.einsum("nhd,kd->hnk", cotangent, own_values, preferred_element_type=jnp.float32)
    dscores = prob_full * (dprobs - attn_delta[:, :, None])
    grad_value = jnp.einsum(
        "hnk,nhd->kd", prob_full, cotangent.astype(jnp.float32), precision=HIGHEST
    )
    grad_key = (
        jnp.einsum("hnk,nhd->kd", dscores, queries.astype(jnp.float32), precision=HIGHEST)
        * score_scale
    )
    slot_mask = (jnp.arange(KV_HEADS) == kv_group)[None, :, None]
    key_slots = jnp.where(slot_mask, grad_key[:, None, :], 0.0).reshape(tok_rows, KV_HEADS * HD)
    value_slots = jnp.where(slot_mask, grad_value[:, None, :], 0.0).reshape(tok_rows, KV_HEADS * HD)
    attn_dk, attn_dv = lax.psum((key_slots, value_slots), "head")
    raw_inputs = (
        gdn_q.astype(jnp.float32),
        gdn_k.astype(jnp.float32),
        gdn_v.astype(jnp.float32),
        decay_logit,
        write_logit,
    )
    value_heads = gdn_v.shape[1] // GDIM
    zero_memory = jnp.zeros((value_heads, GDIM, GDIM), jnp.float32)
    unit_memory = jnp.broadcast_to(jnp.eye(GDIM, dtype=jnp.float32), zero_memory.shape)

    def local_run(raw_values, memory):
        return delta_forward(raw_values, memory, decay_rate, write_scale)

    silent_inputs = (
        raw_inputs[0],
        raw_inputs[1],
        jnp.zeros_like(raw_inputs[2]),
        raw_inputs[3],
        raw_inputs[4],
    )
    transition = local_run(silent_inputs, unit_memory)[1]
    outputs_zero, pull_zero = jax.vjp(local_run, raw_inputs, zero_memory)
    written_end = outputs_zero[1]
    cot_full = gdn_cot.astype(jnp.float32)
    local_grad = pull_zero((cot_full, zero_memory))[1]
    memory_in = prefix(
        (transition, written_end), "ctx", compose_maps, (unit_memory, zero_memory), False
    )[1]
    flipped = jnp.swapaxes(transition, 1, 2)
    memory_grad = prefix(
        (flipped, local_grad), "ctx", compose_maps, (unit_memory, zero_memory), True
    )[1]
    unused_out, pull_final = jax.vjp(local_run, raw_inputs, memory_in)
    grads = pull_final((cot_full, memory_grad))[0]
    return (grad_q, attn_dk, attn_dv, grads[0], grads[1], grads[2], grads[3], grads[4])


def solution(mesh):
    return jax.shard_map(
        on_device,
        mesh=mesh,
        in_specs=(
            P("ctx", "head"),
            P("ctx", None),
            P("ctx", None),
            P("ctx", "head"),
            P("head", None),
            P("head", None),
            P("head", None, None),
            P("ctx", "head"),
            P("ctx", "head"),
            P("ctx", "head"),
            P("head", "ctx"),
            P("head", "ctx"),
            P("head"),
            P("head"),
            P("ctx", "head"),
        ),
        out_specs=(
            P("ctx", "head"),
            P("ctx", None),
            P("ctx", None),
            P("ctx", "head"),
            P("ctx", "head"),
            P("ctx", "head"),
            P("head", "ctx"),
            P("head", "ctx"),
        ),
        check_vma=False,
    )
```

profile of v0, /device:TPU:0, one launch (start us, length us, event | category | flops | bytes accessed | tf_op | source)
XLA Modules:
  0.0 837.9 jit_solution(16207769356477469566)
XLA Ops:
  17.1 91.2 %while.177 = (s32[]{:T(128)}, f32[8,128,128]{2,1,0:T(8,128)S(1)}, f32[2,8,64,1]{2,1,3,0:T(8,128)S(1)}, f32[2,8,64,1]{2,1,3,0:T(8,128)S(1)}, f32[2,8,64,64]{3,2,1...) while((s32[]{:T(128)}, f32[8,128,128]{2,1,0:T(8,128)S(1)}, ...), condition=%wide.region_11.13_spmd.clone.clone, body=%wide.region_9.12_spmd.clone.clone.sunk | while | flops 353555008 | bytes 9751032 | solution.py:92
  20.1 39.3 %custom-call.48 = f32[8,1,64,64]{2,3,1,0:T(8,128)S(1)} custom-call(f32[8,1,64,64]{3,2,1,0:T(8,128)S(1)} %add_bitcast_fusion.8), custom_call_target="InvertDiagBlocksLowerTriangular" | custom-call | tf_op jit(solution)/shard_map/jvp()/while/body/eval_jaxpr/triangular_solve/custom-call.1 | solution.py:54
  65.7 39.3 %custom-call.48 = f32[8,1,64,64]{2,3,1,0:T(8,128)S(1)} custom-call(f32[8,1,64,64]{3,2,1,0:T(8,128)S(1)} %add_bitcast_fusion.8), custom_call_target="InvertDiagBlocksLowerTriangular" | custom-call | tf_op jit(solution)/shard_map/jvp()/while/body/eval_jaxpr/triangular_solve/custom-call.1 | solution.py:54
  109.7 89.5 %while.174 = (s32[]{:T(128)}, f32[8,128,128]{2,1,0:T(8,128)S(1)}, f32[2,8,1,1]{1,3,2,0:T(1,128)S(1)}, f32[2,8,64,1]{2,1,3,0:T(8,128)S(1)}, f32[2,8,64,128]{3,2,1...) while((s32[]{:T(128)}, f32[8,128,128]{2,1,0:T(8,128)S(1)}, ...), condition=%wide.region_13.16_spmd.clone, body=%wide.region_12.15_spmd.clone.sunk | while | flops 403779648 | bytes 6229739 | solution.py:92
  112.6 39.3 %custom-call.47 = f32[8,1,64,64]{2,3,1,0:T(8,128)S(1)} custom-call(f32[8,1,64,64]{3,2,1,0:T(8,128)S(1)} %fusion.498), custom_call_target="InvertDiagBlocksLowerTriangular" | custom-call | tf_op jit(solution)/shard_map/transpose(jvp())/while/body/eval_jaxpr/triangular_solve/custom-call.0 | solution.py:54
  157.3 39.3 %custom-call.47 = f32[8,1,64,64]{2,3,1,0:T(8,128)S(1)} custom-call(f32[8,1,64,64]{3,2,1,0:T(8,128)S(1)} %fusion.498), custom_call_target="InvertDiagBlocksLowerTriangular" | custom-call | tf_op jit(solution)/shard_map/transpose(jvp())/while/body/eval_jaxpr/triangular_solve/custom-call.0 | solution.py:54
  200.1 10.5 %all-gather.17.cloned.1.call-start = ((), (), s32[]{:S(2)}) async-start(), calls=%async_computation.2 | async-start | bytes 4718592 | tf_op jit(solution)/shard_map/all_gather | solution.py:20
  210.6 86.8 %while.171 = (s32[]{:T(128)}, f32[8,128,128]{2,1,0:T(8,128)S(1)}, f32[2,8,64]{2,1,0:T(8,128)S(1)}, f32[2,8,64]{2,1,0:T(8,128)S(1)}, f32[2,8,64,128]{3,2,1,0:T(8,128)S(1)}, /*index=5*/s32[]{:T(128)}, f32[]{:T(128)}) while((s32[]{:T(128)}, f32[8,128,128]{2,1,0:T(8,128)S(1)}, f32[2,8,64]{2,1,0:T(8,128)S(1)}, f32[2,8,64]{2,1,0:T(8,128)S(1)}, ...), condition=%wide.region_7.9_spmd, body=%wide.region_5.8_spmd.sunk | while | flops 302833728 | bytes 3835137 | solution.py:92
  213.0 39.3 %custom-call.43 = f32[8,1,64,64]{2,3,1,0:T(8,128)S(1)} custom-call(f32[8,1,64,64]{3,2,1,0:T(8,128)S(1)} %fusion.435), custom_call_target="InvertDiagBlocksLowerTriangular" | custom-call | tf_op jit(solution)/shard_map/while/body/eval_jaxpr/triangular_solve/custom-call.1 | solution.py:54
  256.4 39.3 %custom-call.43 = f32[8,1,64,64]{2,3,1,0:T(8,128)S(1)} custom-call(f32[8,1,64,64]{3,2,1,0:T(8,128)S(1)} %fusion.435), custom_call_target="InvertDiagBlocksLowerTriangular" | custom-call | tf_op jit(solution)/shard_map/while/body/eval_jaxpr/triangular_solve/custom-call.1 | solution.py:54
  307.0 20.6 %all-gather.1 = bf16[1024,1,256]{0,2,1:T(8,128)(2,1)S(1)} all-gather(bf16[128,1,256]{0,2,1:T(8,128)(2,1)S(1)} %constant_dynamic-slice_fusion.13), channel_id=3, replica_groups=mesh['ctx'=8,'head'=4] {'ctx'}, dimensions={0}, use_global_device_ids=true | all-gather | bytes 589824 | tf_op jit(solution)/shard_map/all_gather | solution.py:202
  327.9 17.1 %all-gather = bf16[1024,1,256]{2,0,1:T(8,128)(2,1)S(1)} all-gather(bf16[128,1,256]{2,0,1:T(8,128)(2,1)} %copy.795), channel_id=2, replica_groups=mesh['ctx'=8,'head'=4] {'ctx'}, dimensions={0}, use_global_device_ids=true | all-gather | bytes 589824 | tf_op jit(solution)/shard_map/all_gather | solution.py:201
  367.4 5.8 copy.738
  388.0 13.7 %while.175 = (s32[]{:T(128)}, f32[8,128,128]{1,2,0:T(8,128)S(1)}, s32[]{:T(128)}, f32[8,8,128,128]{2,3,1,0:T(8,128)}, f32[8,8,128,128]{2,3,1,0:T(8,128)}, /*index=5*/s32[]{:T(128)}, s32[]{:T(128)}) while((s32[]{:T(128)}, f32[8,128,128]{1,2,0:T(8,128)S(1)}, s32[]{:T(128)}, f32[8,8,128,128]{2,3,1,0:T(8,128)}, ...), condition=%wide.region_15.18_spmd.clone, body=%wide.region_14.17_spmd.clone.sunk | while | flops 201850880 | bytes 3672671 | solution.py:32
  404.2 47.4 %all-gather.21.cloned.1.call-done = f32[64,128,128]{2,1,0:T(8,128)} async-done(((f32[8,128,128]{2,1,0:T(8,128)}), f32[64,128,128]{2,1,0:T(8,128)}) %all-gather.21.cloned.1.call-update) | async-done | bytes 4194320 | tf_op jit(solution)/shard_map/all_gather | solution.py:20
  451.6 36.2 %while.176 = (s32[]{:T(128)}, f32[8,128,128]{1,2,0:T(8,128)}, s32[]{:T(128)}, f32[8,8,128,128]{3,2,1,0:T(8,128)}, f32[8,8,128,128]{3,2,1,0:T(8,128)}, /*index=5*/s32[]{:T(128)}, s32[]{:T(128)}) while((s32[]{:T(128)}, f32[8,128,128]{1,2,0:T(8,128)}, s32[]{:T(128)}, f32[8,8,128,128]{3,2,1,0:T(8,128)}, ...), condition=%wide.region_17.20_spmd.clone, body=%wide.region_16.19_spmd.clone.sunk | while | flops 201850880 | bytes 5769315 | solution.py:32
  501.1 111.7 %while.172 = (s32[]{:T(128)}, f32[8,128,128]{2,1,0:T(8,128)S(1)}, f32[2,8,64,64]{3,2,1,0:T(8,128)}, f32[2,8,64,64]{3,2,1,0:T(8,128)}, f32[2,8,64,64]{3,2,1,0:T(8...) while((s32[]{:T(128)}, f32[8,128,128]{2,1,0:T(8,128)S(1)}, ...), condition=%wide.region_20.23_spmd.clone.clone, body=%wide.region_18.22_spmd.clone.clone.sunk | while | flops 454513728 | bytes 36297284 | solution.py:92
  505.2 40.7 %custom-call.44 = f32[8,1,64,64]{2,3,1,0:T(8,128)} custom-call(f32[8,1,64,64]{3,2,1,0:T(8,128)} %add_bitcast_fusion.6), custom_call_target="InvertDiagBlocksLowerTriangular" | custom-call | tf_op jit(solution)/shard_map/jvp()/while/body/eval_jaxpr/triangular_solve/custom-call.1 | solution.py:54
  561.1 40.7 %custom-call.44 = f32[8,1,64,64]{2,3,1,0:T(8,128)} custom-call(f32[8,1,64,64]{3,2,1,0:T(8,128)} %add_bitcast_fusion.6), custom_call_target="InvertDiagBlocksLowerTriangular" | custom-call | tf_op jit(solution)/shard_map/jvp()/while/body/eval_jaxpr/triangular_solve/custom-call.1 | solution.py:54
  615.6 202.5 %while.173 = (s32[]{:T(128)}, f32[8,128,128]{2,1,0:T(8,128)S(1)}, f32[2,8,64,128]{3,2,0,1:T(8,128)}, f32[2,8,64,128]{3,2,0,1:T(8,128)}, f32[2,8,64,128]{3,2,1,0:...) while((s32[]{:T(128)}, f32[8,128,128]{2,1,0:T(8,128)S(1)}, ...), condition=%wide.region_32.35_spmd.clone.clone, body=%wide.region_21.34_spmd.clone.clone.sunk | while | flops 1034992192 | bytes 34533784 | solution.py:92
  620.9 40.0 %custom-call.46 = f32[8,1,64,64]{2,3,1,0:T(8,128)} custom-call(f32[8,1,64,64]{3,2,1,0:T(8,128)S(1)} %add_bitcast_fusion.7), custom_call_target="InvertDiagBlocksLowerTriangular" | custom-call | tf_op jit(solution)/shard_map/transpose(jvp())/while/body/eval_jaxpr/triangular_solve | solution.py:54
  664.0 39.3 %custom-call.45 = f32[8,1,64,64]{2,3,1,0:T(8,128)S(1)} custom-call(f32[8,1,64,64]{3,2,1,0:T(8,128)S(1)} %fusion.474), custom_call_target="InvertDiagBlocksLowerTriangular" | custom-call | tf_op jit(solution)/shard_map/transpose(jvp())/while/body/eval_jaxpr/triangular_solve/custom-call.0 | solution.py:54
  722.0 40.0 %custom-call.46 = f32[8,1,64,64]{2,3,1,0:T(8,128)} custom-call(f32[8,1,64,64]{3,2,1,0:T(8,128)S(1)} %add_bitcast_fusion.7), custom_call_target="InvertDiagBlocksLowerTriangular" | custom-call | tf_op jit(solution)/shard_map/transpose(jvp())/while/body/eval_jaxpr/triangular_solve | solution.py:54
  765.2 39.3 %custom-call.45 = f32[8,1,64,64]{2,3,1,0:T(8,128)S(1)} custom-call(f32[8,1,64,64]{3,2,1,0:T(8,128)S(1)} %fusion.474), custom_call_target="InvertDiagBlocksLowerTriangular" | custom-call | tf_op jit(solution)/shard_map/transpose(jvp())/while/body/eval_jaxpr/triangular_solve/custom-call.0 | solution.py:54
  (632 shorter events, 243.1 us)
Async XLA Ops:
  7.2 347.8 %all-gather.13.cloned.1.call-start = ((), (), s32[]{:S(2)}) async-start(), calls=%async_computation | async-start | bytes 2359296 | tf_op jit(solution)/shard_map/all_gather | solution.py:228
  9.0 4.3 copy-start.54
  9.0 349.8 %all-gather.15.cloned.1.call-start = ((), (), s32[]{:S(2)}) async-start(), calls=%async_computation.1 | async-start | bytes 2359296 | tf_op jit(solution)/shard_map/all_gather | solution.py:231
  10.9 356.5 %all-gather.19.cloned.1.call-start = ((), (), s32[]{:S(2)}) async-start(), calls=%async_computation.3 | async-start | bytes 4718592 | tf_op jit(solution)/shard_map/all_gather | solution.py:20
  200.1 177.7 %all-gather.17.cloned.1.call-start = ((), (), s32[]{:S(2)}) async-start(), calls=%async_computation.2 | async-start | bytes 4718592 | tf_op jit(solution)/shard_map/all_gather | solution.py:20
  297.5 5.8 copy-start.55
  298.5 105.7 %all-gather.23.cloned.1.call-start = ((), (), s32[]{:S(2)}) async-start(), calls=%async_computation.5 | async-start | bytes 4718592 | tf_op jit(solution)/shard_map/all_gather | solution.py:20
  299.1 152.5 %all-gather.21.cloned.1.call-start = ((), (), s32[]{:S(2)}) async-start(), calls=%async_computation.4 | async-start | bytes 4718592 | tf_op jit(solution)/shard_map/all_gather | solution.py:20
  299.7 527.8 %all-reduce.5.cloned.1.call-start = ((), (), s32[]{:S(2)}) async-start(), calls=%async_computation.6 | async-start | bytes 1048576 | tf_op jit(solution)/shard_map/psum | solution.py:254
  494.2 6.9 copy-start.7
  545.9 4.6 copy-start.3
  545.9 5.9 copy-start.29
  601.8 4.7 copy-start.3
  601.8 6.0 copy-start.29
  615.6 203.6 %copy-start.59 = (f32[128,4]{0,1:T(4,128)S(1)}, f32[128,4]{0,1:T(4,128)}, u32[]{:S(2)}) copy-start(f32[128,4]{0,1:T(4,128)} %copy-done.58) | copy-start | bytes 6148
  615.8 5.1 copy-start.12
  704.5 5.9 copy-start.15
  716.9 5.0 copy-start.12
  805.6 5.9 copy-start.15
  818.0 4.3 copy-start.39
  818.0 4.3 copy-start.61
  818.0 4.3 copy-start.69
  818.0 4.6 copy-start.64
  818.0 4.8 copy-start.44
  (93 other events, 199.6 us)
Sparse Core Ops, SparseCore 0:
  10.2 35.3 all-gather.12
  47.7 30.5 all-gather.14
  200.2 49.9 all-gather.18
  298.6 58.1 all-gather.16
  358.2 45.8 all-gather.22
  405.6 45.9 all-gather.20
  455.1 44.1 all-reduce.4
where the time goes:
time: 848 us; the launch traced here: 838 us
  other arithmetic  501 us (59%)
  matrix products  124 us (15%)
  local copies, waits for them, and re-layouts  95.8 us (11%)
  waiting for transfers between devices  50.9 us (6%)
  blocking collectives  37.8 us (4%)
  between operations  15.3 us (2%)
  starting transfers between devices  10.7 us (1%)
    another operation x44, other arithmetic, span_update(): lax.linalg.triangular_solve(system, target, left_side=True, lower=True, u...  481 us
    all_gather x4, waiting for transfers between devices, prefix(): pieces = jax.tree.map(lambda part: lax.all_gather(part, axis), value)  49.7 us
    dot_general x14, matrix products, compose_maps(): jnp.einsum('hij,hjk->hik', earlier[1], later[0], precision=HIGHEST)  33.1 us
    all_gather x1, blocking collectives, on_device(): lax.all_gather(own_values, 'ctx', axis=0, tiled=True)  20.6 us
    unnamed x122, local copies, waits for them, and re-layouts  17.6 us
    all_gather x1, blocking collectives, on_device(): lax.all_gather(own_keys, 'ctx', axis=0, tiled=True)  17.1 us
  transfers between devices with their start and end apart: 7, of which 2 were waited for; matrix products, arithmetic and copies ran while one was open for 84% of the time, Pallas kernels for 0%

commit v1 on v0

v1 whole, which is shorter than its diff:
```python
import jax
import jax.numpy as jnp
from jax import lax
from jax.experimental import pallas as pl
from jax.experimental.pallas import tpu as pltpu
from jax.sharding import PartitionSpec as P

Q_HEADS = 16
KV_HEADS = 2
HD = 256
GDIM = 128
BLK = 64
TOPK = 4
F32 = jnp.float32
BF16 = jnp.bfloat16
VMEM_BYTES = 48 * 1024 * 1024
MESH = pl.DeviceIdType.MESH


def split(x):
    if x.dtype == BF16:
        return (x, None)
    head = x.astype(BF16)
    return (head, (x - head.astype(F32)).astype(BF16))


def mm(a, b, ca=1, cb=0):
    dims = (((ca,), (cb,)), ((), ()))
    out = lax.dot_general(a[0], b[0], dims, preferred_element_type=F32)
    if b[1] is not None:
        out = out + lax.dot_general(a[0], b[1], dims, preferred_element_type=F32)
    if a[1] is not None:
        out = out + lax.dot_general(a[1], b[0], dims, preferred_element_type=F32)
    return out


def lane_cumsum(x, backward):
    width = x.shape[1]
    lanes = lax.broadcasted_iota(jnp.int32, x.shape, 1)
    step = 1
    while step < width:
        moved = pltpu.roll(x, width - step if backward else step, 1)
        keep = lanes < width - step if backward else lanes >= step
        x = x + jnp.where(keep, moved, 0.0)
        step *= 2
    return x


def softplus(x):
    return jnp.maximum(x, 0.0) + jnp.log(1.0 + jnp.exp(-jnp.abs(x)))


def sigmoid(x):
    return 1.0 / (1.0 + jnp.exp(-x))


def column_form(row, size):
    return jnp.broadcast_to(row, (size, size)).T


def unit_rows(raw):
    full = raw.astype(F32)
    scale = lax.rsqrt(jnp.sum(full * full, axis=-1, keepdims=True) + 1e-06)
    return full * scale, scale


def head_cols(ref, head):
    return ref[:, head * GDIM : (head + 1) * GDIM]


def triangles(size):
    rows = lax.broadcasted_iota(jnp.int32, (size, size), 0)
    cols = lax.broadcasted_iota(jnp.int32, (size, size), 1)
    return rows, cols


def gdn_local(
    q_ref, k_ref, v_ref, cot_ref, decay_ref, write_ref, rate_ref, scale_ref,
    inv_ref, wu_ref, map_ref, mapt_ref, add_ref, pull_ref, gam_ref, beta_ref,
):
    size = q_ref.shape[0]
    key_heads = q_ref.shape[1] // GDIM
    value_heads = v_ref.shape[1] // GDIM
    ratio = value_heads // key_heads
    gam = lane_cumsum(-rate_ref[...] * softplus(decay_ref[...]), False)
    beta = scale_ref[...] * sigmoid(write_ref[...])
    gam_ref[...] = gam
    beta_ref[...] = beta
    rows, cols = triangles(size)
    eye = jnp.where(rows == cols, 1.0, 0.0)
    group = min(4, value_heads)
    for first in range(0, value_heads, group):
        heads = list(range(first, first + group))
        keyed = {}
        for m in sorted({v // ratio for v in heads}):
            qn, kn = unit_rows(head_cols(q_ref, m))[0], unit_rows(head_cols(k_ref, m))[0]
            qs, ks = split(qn), split(kn)
            keyed[m] = (qn, kn, mm(ks, ks, 1, 1), mm(qs, ks, 1, 1), split(kn.T))
        gcol = [column_form(gam[v : v + 1, :], size) for v in heads]
        bcol = [column_form(beta[v : v + 1, :], size) for v in heads]
        upto = [
            jnp.where(rows >= cols, jnp.exp(jnp.minimum(c - gam[v : v + 1, :], 0.0)), 0.0)
            for c, v in zip(gcol, heads)
        ]
        system = [
            jnp.where(rows > cols, b * u * keyed[v // ratio][2], 0.0)
            for b, u, v in zip(bcol, upto, heads)
        ]
        inverse = [eye - jnp.where(rows // 2 == cols // 2, s, 0.0) for s in system]
        half = 2
        while half < size:
            low = (rows // half == cols // half + 1) & ((rows // half) % 2 == 1)
            parts = [split(t) for t in inverse]
            inner = [mm(split(jnp.where(low, s, 0.0)), t) for s, t in zip(system, parts)]
            outer = [mm(t, split(x)) for t, x in zip(parts, inner)]
            inverse = [t - x for t, x in zip(inverse, outer)]
            half *= 2
        for n, v in enumerate(heads):
            qn, kn, gram, cross, knt = keyed[v // ratio]
            now = jnp.exp(gcol[n])
            inv_ref[v] = inverse[n]
            targets = jnp.concatenate(
                [bcol[n] * now * kn, bcol[n] * head_cols(v_ref, v).astype(F32)], axis=1
            )
            wu = mm(split(inverse[n]), split(targets))
            wu_ref[v] = wu
            last = gam[v : v + 1, size - 1 : size]
            tail = jnp.exp(last - gcol[n])
            ends = mm(knt, split(jnp.concatenate([tail, tail], axis=1) * wu))
            whole = jnp.exp(last) * eye - ends[:, :GDIM]
            map_ref[v] = whole
            mapt_ref[v] = whole.T
            add_ref[v] = ends[:, GDIM:]
            reads = now * qn - mm(split(upto[n] * cross), split(wu[:, :GDIM]))
            pull_ref[v] = mm(split(reads.T), split(head_cols(cot_ref, v)))


def gdn_chain(
    map_ref, mapt_ref, add_ref, pull_ref, mem_ref, grad_ref,
    mem_in, mem_out, grad_in, grad_out, mem_send, mem_recv, grad_send, grad_recv,
):
    n = lax.axis_size("ctx")
    me = lax.axis_index("ctx")
    head_at = lax.axis_index("head")
    heads = map_ref.shape[0]
    right, left = lax.rem(me + 1, n), lax.rem(me + n - 1, n)
    barrier = pltpu.get_barrier_semaphore()
    for neighbour in (left, right):
        pl.semaphore_signal(barrier, inc=1, device_id=(neighbour, head_at), device_id_type=MESH)
    pl.semaphore_wait(barrier, 2)

    def send(source, target, send_sem, recv_sem, head, to):
        return pltpu.make_async_remote_copy(
            src_ref=source.at[head],
            dst_ref=target.at[head],
            send_sem=send_sem.at[head],
            recv_sem=recv_sem.at[head],
            device_id=(to, head_at),
            device_id_type=MESH,
        )

    def advance(head):
        copy = send(mem_out, mem_in, mem_send, mem_recv, head, right)

        @pl.when(me == 0)
        def _():
            mem_in[head] = jnp.zeros((GDIM, GDIM), F32)

        @pl.when(me > 0)
        def _():
            copy.wait_recv()

        @pl.when(me < n - 1)
        def _():
            mem_out[head] = mm(split(map_ref[head]), split(mem_in[head])) + add_ref[head]
            copy.start()

    def retreat(head):
        copy = send(grad_out, grad_in, grad_send, grad_recv, head, left)

        @pl.when(me == n - 1)
        def _():
            grad_in[head] = jnp.zeros((GDIM, GDIM), F32)

        @pl.when(me < n - 1)
        def _():
            copy.wait_recv()

        @pl.when(me > 0)
        def _():
            grad_out[head] = mm(split(mapt_ref[head]), split(grad_in[head])) + pull_ref[head]
            copy.start()

    lag = jnp.clip((n - 1 - 2 * me) * 3, -heads, heads)
    mem_late, grad_late = jnp.maximum(-lag, 0), jnp.maximum(lag, 0)

    def turn(step, carry):
        mem_head, grad_head = step - mem_late, step - grad_late

        @pl.when((mem_head >= 0) & (mem_head < heads))
        def _():
            advance(mem_head)

        @pl.when((grad_head >= 0) & (grad_head < heads))
        def _():
            retreat(grad_head)

        return carry

    lax.fori_loop(0, 2 * heads, turn, 0)

    def drain(head, carry):
        @pl.when(me < n - 1)
        def _():
            send(mem_out, mem_in, mem_send, mem_recv, head, right).wait_send()

        @pl.when(me > 0)
        def _():
            send(grad_out, grad_in, grad_send, grad_recv, head, left).wait_send()

        return carry

    lax.fori_loop(0, heads, drain, 0)
    mem_ref[...] = mem_in[...]
    grad_ref[...] = grad_in[...]


def gdn_grads(
    q_ref, k_ref, v_ref, cot_ref, decay_ref, write_ref, rate_ref, scale_ref,
    inv_ref, wu_ref, gam_ref, beta_ref, mem_ref, grad_ref,
    dq_ref, dk_ref, dv_ref, ddecay_ref, dwrite_ref,
):
    size = q_ref.shape[0]
    key_heads = q_ref.shape[1] // GDIM
    value_heads = v_ref.shape[1] // GDIM
    ratio = value_heads // key_heads
    rows, cols = triangles(size)
    gam, beta = gam_ref[...], beta_ref[...]
    dgam_rows, dbeta_rows, ends = [], [], []
    for m in range(key_heads):
        heads = list(range(m * ratio, (m + 1) * ratio))
        qn, qscale = unit_rows(head_cols(q_ref, m))
        kn, kscale = unit_rows(head_cols(k_ref, m))
        qs, ks = split(qn), split(kn)
        gram, cross = mm(ks, ks, 1, 1), mm(qs, ks, 1, 1)
        gcol = [column_form(gam[v : v + 1, :], size) for v in heads]
        bcol = [column_form(beta[v : v + 1, :], size) for v in heads]
        lasts = [gam[v : v + 1, size - 1 : size] for v in heads]
        now = [jnp.exp(c) for c in gcol]
        tail = [jnp.exp(e - c) for e, c in zip(lasts, gcol)]
        upto = [
            jnp.where(rows >= cols, jnp.exp(jnp.minimum(c - gam[v : v + 1, :], 0.0)), 0.0)
            for c, v in zip(gcol, heads)
        ]
        strict = [jnp.where(rows > cols, u, 0.0) for u in upto]
        mem = [mem_ref[v] for v in heads]
        grad = [grad_ref[v] for v in heads]
        mems, grads = [split(x) for x in mem], [split(x) for x in grad]
        cots = [split(head_cols(cot_ref, v)) for v in heads]
        written = [
            wu_ref[v][:, GDIM:] - mm(split(wu_ref[v][:, :GDIM]), s) for v, s in zip(heads, mems)
        ]
        ws = [split(w) for w in written]
        dwritten = [
            mm(split((u * cross).T), c) + t * mm(ks, g)
            for u, c, t, g in zip(upto, cots, tail, grads)
        ]
        target = [mm(split(inv_ref[v].T), split(d)) for v, d in zip(heads, dwritten)]
        xs = [split(x) for x in target]
        dcross = [u * mm(c, w, 1, 1) for u, c, w in zip(upto, cots, ws)]
        dsys = [-s * mm(x, w, 1, 1) for s, x, w in zip(strict, xs, ws)]
        dgram = [b * d for b, d in zip(bcol, dsys)]
        zq = [e * mm(c, s, 1, 1) for e, c, s in zip(now, cots, mems)]
        zk = [-e * mm(x, s, 1, 1) for e, x, s in zip(now, xs, mems)]
        wg = [t * mm(w, g, 1, 1) for t, w, g in zip(tail, ws, grads)]
        dqn, dkn = None, None
        cross_sum, gram_sum = dcross[0], dgram[0]
        dqn, dkn = zq[0], bcol[0] * zk[0] + wg[0]
        for n in range(1, ratio):
            cross_sum, gram_sum = cross_sum + dcross[n], gram_sum + dgram[n]
            dqn, dkn = dqn + zq[n], dkn + bcol[n] * zk[n] + wg[n]
        dqn = dqn + mm(split(cross_sum), ks)
        dkn = dkn + mm(split(cross_sum.T), qs) + mm(split(gram_sum + gram_sum.T), ks)
        for raw, scale, dn, out in ((qn, qscale, dqn, dq_ref), (kn, kscale, dkn, dk_ref)):
            along = jnp.sum(raw * dn, axis=-1, keepdims=True)
            out[:, m * GDIM : (m + 1) * GDIM] = scale * (dn - raw * along)
        for n, v in enumerate(heads):
            dv_ref[:, v * GDIM : (v + 1) * GDIM] = bcol[n] * target[n]
            pairs = dcross[n] * cross + dgram[n] * gram
            kept = kn * wg[n]
            old = kn * zk[n]
            by_row = pairs + qn * zq[n] + bcol[n] * old - kept
            dgam_rows.append(jnp.sum(by_row.T - pairs, axis=0, keepdims=True))
            values = head_cols(v_ref, v).astype(F32)
            by_beta = dsys[n] * gram + target[n] * values + old
            dbeta_rows.append(jnp.sum(by_beta.T, axis=0, keepdims=True))
            both = kept + jnp.exp(lasts[n]) * (mem[n] * grad[n])
            ends.append(jnp.sum(jnp.sum(both, axis=0, keepdims=True), axis=1, keepdims=True))
    dlog = lane_cumsum(jnp.concatenate(dgam_rows, axis=0), True) + jnp.concatenate(ends, axis=0)
    dbeta = jnp.concatenate(dbeta_rows, axis=0)
    ddecay_ref[...] = -rate_ref[...] * sigmoid(decay_ref[...]) * dlog
    gate = sigmoid(write_ref[...])
    dwrite_ref[...] = scale_ref[...] * gate * (1.0 - gate) * dbeta


def attention(lists_ref, q_ref, cot_ref, lse_ref, delta_ref, k_ref, v_ref, dq_ref, dkv_ref):
    score_scale = HD ** (-0.5)
    step = pl.program_id(0)
    tokens = q_ref.shape[0]
    heads = q_ref.shape[1] // HD
    keys = k_ref.shape[0]
    blocks_here = tokens // BLK
    n_blocks = lists_ref.shape[0] // (heads * TOPK)
    first = lax.axis_index("ctx") * blocks_here

    def stacked(ref):
        return jnp.concatenate([ref[:, h * HD : (h + 1) * HD] for h in range(heads)], axis=0)

    q, cot = stacked(q_ref), stacked(cot_ref)
    k, v = k_ref[...], v_ref[...]
    key_pos = step * keys + lax.broadcasted_iota(jnp.int32, (keys, tokens), 0)
    key_block = key_pos // BLK
    lane = lax.broadcasted_iota(jnp.int32, (1, tokens), 1)
    row_pos = first * BLK + lane
    row_block = row_pos // BLK
    own = (key_block == row_block) & (key_pos <= row_pos)
    before = key_block < row_block
    allowed = []
    for h in range(heads):
        member = None
        for t in range(TOPK):
            entry = jnp.zeros((1, tokens), jnp.int32)
            for b in range(blocks_here):
                listed = lists_ref[(h * n_blocks + first + b) * TOPK + t]
                entry = jnp.where(lane // BLK == b, listed, entry)
            hit = key_block == entry
            member = hit if member is None else member | hit
        allowed.append(own | (before & member))
    scores = mm((k, None), (q, None), 1, 1)
    dprobs = mm((v, None), (cot, None), 1, 1)
    probs, dscores = [], []
    for h in range(heads):
        span = slice(h * tokens, (h + 1) * tokens)
        mine = pl.ds(pl.multiple_of(first * BLK, tokens), tokens)
        lse, delta = lse_ref[h : h + 1, mine], delta_ref[h : h + 1, mine]
        prob = jnp.where(allowed[h], jnp.exp(scores[:, span] * score_scale - lse), 0.0)
        probs.append(prob)
        dscores.append(prob * (dprobs[:, span] - delta) * score_scale)
    ds = split(jnp.concatenate(dscores, axis=1))
    dkv_ref[:, :HD] = mm(ds, (q, None))
    dkv_ref[:, HD:] = mm(split(jnp.concatenate(probs, axis=1)), (cot, None))
    dq = mm(ds, (k, None), 0, 0)

    @pl.when(step == 0)
    def _():
        dq_ref[...] = jnp.zeros_like(dq_ref)

    for h in range(heads):
        dq_ref[:, h * HD : (h + 1) * HD] += dq[h * tokens : (h + 1) * tokens]


def on_device(
    attn_q, attn_k, attn_v, attn_cot, attn_lse, attn_delta, block_lists,
    gdn_q, gdn_k, gdn_v, decay_logit, write_logit, decay_rate, write_scale, gdn_cot,
):
    tokens = attn_q.shape[0]
    local_heads = attn_q.shape[1] // HD
    ctx = lax.axis_size("ctx")
    head_devices = lax.axis_size("head")
    n_rows = tokens * ctx
    kv_group = lax.axis_index("head") * local_heads // (Q_HEADS // KV_HEADS)
    own_kv = jnp.concatenate(
        [
            lax.dynamic_slice_in_dim(attn_k, kv_group * HD, HD, 1),
            lax.dynamic_slice_in_dim(attn_v, kv_group * HD, HD, 1),
        ],
        axis=1,
    )
    all_kv = lax.all_gather(own_kv, "ctx", axis=0, tiled=True)

    value_heads = gdn_v.shape[1] // GDIM
    rates, scales = decay_rate[:, None], write_scale[:, None]
    vmem = pl.BlockSpec(memory_space=pltpu.VMEM)
    square = jax.ShapeDtypeStruct((value_heads, GDIM, GDIM), F32)
    gates = jax.ShapeDtypeStruct((value_heads, tokens), F32)
    inverse, wu, maps, maps_t, adds, pulls, gam, beta = pl.pallas_call(
        gdn_local,
        out_shape=(
            jax.ShapeDtypeStruct((value_heads, tokens, tokens), F32),
            jax.ShapeDtypeStruct((value_heads, tokens, 2 * GDIM), F32),
            square, square, square, square, gates, gates,
        ),
        in_specs=[vmem] * 8,
        out_specs=[vmem] * 8,
        compiler_params=pltpu.CompilerParams(vmem_limit_bytes=VMEM_BYTES),
        name="gdn_local",
    )(gdn_q, gdn_k, gdn_v, gdn_cot, decay_logit, write_logit, rates, scales)

    keys = min(256, n_rows)
    grad_q, dkv = pl.pallas_call(
        attention,
        grid=(n_rows // keys,),
        out_shape=(
            jax.ShapeDtypeStruct((tokens, local_heads * HD), F32),
            jax.ShapeDtypeStruct((n_rows, 2 * HD), F32),
        ),
        in_specs=[
            pl.BlockSpec(memory_space=pltpu.SMEM),
            vmem, vmem, vmem, vmem,
            pl.BlockSpec((keys, HD), lambda i: (i, 0)),
            pl.BlockSpec((keys, HD), lambda i: (i, 1)),
        ],
        out_specs=(
            pl.BlockSpec((tokens, local_heads * HD), lambda i: (0, 0)),
            pl.BlockSpec((keys, 2 * HD), lambda i: (i, 0)),
        ),
        compiler_params=pltpu.CompilerParams(vmem_limit_bytes=VMEM_BYTES),
        name="attention",
    )(block_lists.reshape(-1), attn_q, attn_cot, attn_lse, attn_delta, all_kv, all_kv)

    mine = lax.psum_scatter(dkv, "ctx", scatter_dimension=0, tiled=True)
    groups = lax.all_gather(mine, "head", axis=0)
    groups = groups.reshape(KV_HEADS, head_devices // KV_HEADS, tokens, 2 * HD).sum(axis=1)
    attn_dk = jnp.concatenate([groups[c, :, :HD] for c in range(KV_HEADS)], axis=1)
    attn_dv = jnp.concatenate([groups[c, :, HD:] for c in range(KV_HEADS)], axis=1)

    buffer = pltpu.VMEM((value_heads, GDIM, GDIM), F32)
    sems = pltpu.SemaphoreType.DMA((value_heads,))
    mem, grad = pl.pallas_call(
        gdn_chain,
        out_shape=(square, square),
        in_specs=[vmem] * 4,
        out_specs=(vmem, vmem),
        scratch_shapes=[buffer] * 4 + [sems] * 4,
        compiler_params=pltpu.CompilerParams(
            collective_id=0, has_side_effects=True, vmem_limit_bytes=VMEM_BYTES
        ),
        name="gdn_chain",
    )(maps, maps_t, adds, pulls)

    dq, dk, dv, ddecay, dwrite = pl.pallas_call(
        gdn_grads,
        out_shape=(
            jax.ShapeDtypeStruct(gdn_q.shape, F32),
            jax.ShapeDtypeStruct(gdn_k.shape, F32),
            jax.ShapeDtypeStruct(gdn_v.shape, F32),
            gates, gates,
        ),
        in_specs=[vmem] * 14,
        out_specs=[vmem] * 5,
        compiler_params=pltpu.CompilerParams(vmem_limit_bytes=VMEM_BYTES),
        name="gdn_grads",
    )(
        gdn_q, gdn_k, gdn_v, gdn_cot, decay_logit, write_logit, rates, scales,
        inverse, wu, gam, beta, mem, grad,
    )
    return (grad_q, attn_dk, attn_dv, dq, dk, dv, ddecay, dwrite)


def solution(mesh):
    return jax.shard_map(
        on_device,
        mesh=mesh,
        in_specs=(
            P("ctx", "head"), P("ctx", None), P("ctx", None), P("ctx", "head"),
            P("head", None), P("head", None), P("head", None, None),
            P("ctx", "head"), P("ctx", "head"), P("ctx", "head"),
            P("head", "ctx"), P("head", "ctx"), P("head"), P("head"), P("ctx", "head"),
        ),
        out_specs=(
            P("ctx", "head"), P("ctx", None), P("ctx", None),
            P("ctx", "head"), P("ctx", "head"), P("ctx", "head"),
            P("head", "ctx"), P("head", "ctx"),
        ),
        check_vma=False,
    )
```

time: 848 us -> 131 us (0.15); the launches traced: 838 us -> 130 us
  other arithmetic: 501 us -> 3.48 us
  matrix products: 124 us -> 0 us
  local copies, waits for them, and re-layouts: 95.8 us -> 6.58 us
  Pallas kernels: 0 us -> 45.2 us
  blocking collectives: 37.8 us -> 0 us
  starting transfers between devices: 10.7 us -> 0.12 us
  waiting for transfers between devices: 50.9 us -> 60.8 us
    another operation x55 -> x0, other arithmetic: 483 us -> none  [the longest x44 481 us: span_update(): lax.linalg.triangular_solve(system, target, left_side=True, lower=True, u...]
    dot_general x82 -> x0, matrix products: 109 us -> none  [the longest x14 33.1 us: compose_maps(): jnp.einsum('hij,hjk->hik', earlier[1], later[0], precision=HIGHEST)]
    pallas_call x0 -> x4, Pallas kernels: none -> 45.2 us  [the longest x1 22.6 us: on_device(): pl.pallas_call(gdn_chain, out_shape=(square, square), in_specs=[vmem] * 4...]
    all_gather x2 -> x0, blocking collectives: 37.8 us -> none  [the longest x1 20.6 us: on_device(): lax.all_gather(own_values, 'ctx', axis=0, tiled=True)]
    reduce_scatter x0 -> x1, waiting for transfers between devices: none -> 35.5 us  [on_device(): mine = lax.psum_scatter(dkv, 'ctx', scatter_dimension=0, tiled=True)]
    all_gather x6 -> x2, waiting for transfers between devices: 49.7 us -> 25.2 us  [the longest x1 25.2 us: on_device(): all_kv = lax.all_gather(own_kv, 'ctx', axis=0, tiled=True)]
    while x136 -> x0, local copies, waits for them, and re-layouts: 16.7 us -> none
    another operation x31 -> x0, local copies, waits for them, and re-layouts: 15.6 us -> none
  transfers between devices with their start and end apart: 7 -> 3, of which waited for: 2 -> 2; matrix products, arithmetic and copies ran while one was open for 84% -> 1% of each run, Pallas kernels for 0% -> 30%
where the time goes in v1:
time: 131 us; the launch traced here: 130 us
  waiting for transfers between devices  60.8 us (46%)
  Pallas kernels  45.2 us (35%)
  between operations  13.9 us (11%)
  local copies, waits for them, and re-layouts  6.58 us (5%)
  other arithmetic  3.48 us (3%)
    reduce_scatter x1, waiting for transfers between devices, on_device(): mine = lax.psum_scatter(dkv, 'ctx', scatter_dimension=0, tiled=True)  35.5 us
    all_gather x1, waiting for transfers between devices, on_device(): all_kv = lax.all_gather(own_kv, 'ctx', axis=0, tiled=True)  25.2 us
    pallas_call x1, Pallas kernels, on_device(): pl.pallas_call(gdn_chain, out_shape=(square, square), in_specs=[vmem] * 4...  22.6 us
    pallas_call x1, Pallas kernels, on_device(): pl.pallas_call(gdn_local, out_shape=(jax.ShapeDtypeStruct((value_heads, t...  9.58 us
    pallas_call x1, Pallas kernels, on_device(): pl.pallas_call(gdn_grads, out_shape=(jax.ShapeDtypeStruct(gdn_q.shape, F3...  6.73 us
    pallas_call x1, Pallas kernels, on_device(): pl.pallas_call(attention, grid=(n_rows // keys,), out_shape=(jax.ShapeDty...  6.29 us
    unnamed x27, local copies, waits for them, and re-layouts  5.39 us
  transfers between devices with their start and end apart: 3, of which 2 were waited for; matrix products, arithmetic and copies ran while one was open for 1% of the time, Pallas kernels for 30%

profile of v1, /device:TPU:0, one launch (start us, length us, event | category | flops | bytes accessed | tf_op | source)
XLA Modules:
  0.0 130.1 jit_solution(6076360710303587320)
XLA Ops:
  7.2 0.0 all-gather.4.cloned.1.call-start
  7.2 0.9 constant_dynamic-slice_fusion
  8.1 0.7 pad_maximum_fusion.2
  8.8 0.0 reduce-scatter.2.cloned.1.call-start
  8.9 0.8 copy.27
  9.7 0.1 reshape.22.lists_ref
  9.8 25.2 %all-gather.4.cloned.1.call-done.k_ref.v_ref = bf16[1024,512]{1,0:T(8,128)(2,1)} async-done(((bf16[128,512]{1,0:T(8,128)(2,1)}), bf16[1024,512]{1,0:T(8,128)(2,1)}) %all-gather.4.cloned.1.call-update) | async-done | bytes 1048592 | tf_op jit(solution)/shard_map/all_gather | solution.py:379
  35.0 1.2 copy-done
  36.2 0.9 copy-done.5
  37.2 0.9 copy-done.6
  38.1 0.7 copy-done.7
  38.9 0.7 copy-done.8
  39.6 6.3 %attention.1 = (f32[128,1024]{1,0:T(8,128)}, f32[1024,512]{1,0:T(8,128)}) custom-call(s32[256]{0:T(256)S(1)} %reshape.22.lists_ref, bf16[128,1024]{1,0:T(8,128)(2,1)S(1)} %copy-done.5, bf16[128,1024]{1,0:T(8,128)(2,1)S(1)} %copy-done.6, f32[4,1024]{1,0:T(4,128)S(1)} %copy-done.7, f32[4,1024]{1,0:T(4,128)S(1)} %copy-done.8, bf16[1024,512]{1,0:T(8,128)(2,1)S(1)} %copy-done, ...), custom_call_target="tpu_custom_call" | custom-call | tf_op jit(solution)/shard_map/attention/pallas_call | solution.py:400
  45.9 0.0 reduce-scatter.2.cloned.1.call-update
  45.9 0.0 all-gather.6.cloned.1.call-start
  46.0 35.5 %reduce-scatter.2.cloned.1.call-done = f32[128,512]{1,0:T(8,128)} async-done(((f32[1024,512]{1,0:T(8,128)}), f32[128,512]{1,0:T(8,128)}) %reduce-scatter.2.cloned.1.call-update) | async-done | bytes 262160 | tf_op jit(solution)/shard_map/reduce_scatter | solution.py:421
  81.6 0.1 copy.30.rate_ref
  81.7 0.1 copy.31.scale_ref
  81.8 9.6 %gdn_local.1 = (f32[8,128,128]{2,1,0:T(8,128)S(1)}, f32[8,128,256]{2,1,0:T(8,128)S(1)}, f32[8,128,128]{2,1,0:T(8,128)S(1)}, f32[8,128,128]{2,1,0:T(8,128)S(1)}, ...) custom-call(bf16[128,512]{1,0:T(8,128)(2,1)S(1)} %copy-done.3, ...), custom_call_target="tpu_custom_call" | custom-call | tf_op jit(solution)/shard_map/gdn_local/pallas_call | solution.py:386
  91.4 22.6 %gdn_chain.1 = (f32[8,128,128]{2,1,0:T(8,128)S(1)}, f32[8,128,128]{2,1,0:T(8,128)S(1)}) custom-call(f32[8,128,128]{2,1,0:T(8,128)S(1)} %get-tuple-element.31.map_ref, f32[8,128,128]{2,1,0:T(8,128)S(1)} %get-tuple-element.32.mapt_ref, f32[8,128,128]{2,1,0:T(8,128)S(1)} %get-tuple-element.33.add_ref, f32[8,128,128]{2,1,0:T(8,128)S(1)} %get-tuple-element.34.pull_ref), custom_call_target="tpu_custom_call" | custom-call | tf_op jit(solution)/shard_map/gdn_chain/pallas_call | solution.py:429
  113.9 6.7 %gdn_grads.1 = (f32[128,512]{1,0:T(8,128)}, f32[128,512]{1,0:T(8,128)}, f32[128,1024]{1,0:T(8,128)}, f32[8,128]{1,0:T(8,128)}, f32[8,128]{1,0:T(8,128)}) custom-call(bf16[128,512]{1,0:T(8,128)(2,1)S(1)} %copy-done.3, bf16[128,512]{1,0:T(8,128)(2,1)S(1)} %copy-done.4, bf16[128,1024]{1,0:T(8,128)(2,1)S(1)} %copy-done.1, bf16[128,1024]{1,0:T(8,128)(2,1)S(1)} %copy-done.2, ...), custom_call_target="tpu_custom_call" | custom-call | tf_op jit(solution)/shard_map/gdn_grads/pallas_call | solution.py:441
  120.7 1.4 %reduce_sum.9 = f32[2,128,512]{2,1,0:T(8,128)S(1)} reduce(f32[2,2,128,512]{3,2,1,0:T(8,128)} %bitcast.11, f32[]{:T(128)} %constant.28.clone.1), dimensions={1}, to_apply=%region_1.2 | reduce | flops 131072 | bytes 1572868 | tf_op jit(solution)/shard_map/reduce_sum | solution.py:423
  122.1 0.7 pad_maximum_fusion.1
  122.8 0.7 pad_maximum_fusion
  (25 shorter events, 0.1 us)
Async XLA Ops:
  7.2 27.8 %all-gather.4.cloned.1.call-start = ((), (), s32[]{:S(2)}) async-start(), calls=%async_computation.1 | async-start | bytes 1179648 | tf_op jit(solution)/shard_map/all_gather | solution.py:379
  8.8 72.7 %reduce-scatter.2.cloned.1.call-start = ((), (), s32[]{:S(2)}) async-start(), calls=%async_computation.2 | async-start | bytes 2359296 | tf_op jit(solution)/shard_map/reduce_scatter | solution.py:421
  35.0 1.2 copy-start
  36.2 0.9 copy-start.5
  37.2 0.9 copy-start.6
  38.1 0.7 copy-start.7
  38.9 0.7 copy-start.8
  39.6 42.0 %copy-start.11 = (f32[8]{0:T(128)S(1)}, f32[8]{0:T(128)}, u32[]{:S(2)}) copy-start(f32[8]{0:T(128)} %param.27) | copy-start | bytes 100
  39.6 42.1 %copy-start.12 = (f32[8]{0:T(128)S(1)}, f32[8]{0:T(128)}, u32[]{:S(2)}) copy-start(f32[8]{0:T(128)} %param.28) | copy-start | bytes 100
  39.6 42.2 %copy-start.1 = (bf16[128,1024]{1,0:T(8,128)(2,1)S(1)}, bf16[128,1024]{1,0:T(8,128)(2,1)}, u32[]{:S(2)}) copy-start(bf16[128,1024]{1,0:T(8,128)(2,1)} %v_ref.3) | copy-start | bytes 786436
  39.6 42.2 %copy-start.2 = (bf16[128,1024]{1,0:T(8,128)(2,1)S(1)}, bf16[128,1024]{1,0:T(8,128)(2,1)}, u32[]{:S(2)}) copy-start(bf16[128,1024]{1,0:T(8,128)(2,1)} %cot_ref.5) | copy-start | bytes 786436
  39.6 42.2 %copy-start.3 = (bf16[128,512]{1,0:T(8,128)(2,1)S(1)}, bf16[128,512]{1,0:T(8,128)(2,1)}, u32[]{:S(2)}) copy-start(bf16[128,512]{1,0:T(8,128)(2,1)} %q_ref.5) | copy-start | bytes 393220
  39.6 42.2 %copy-start.4 = (bf16[128,512]{1,0:T(8,128)(2,1)S(1)}, bf16[128,512]{1,0:T(8,128)(2,1)}, u32[]{:S(2)}) copy-start(bf16[128,512]{1,0:T(8,128)(2,1)} %k_ref.3) | copy-start | bytes 393220
  39.6 42.1 %copy-start.9 = (f32[8,128]{1,0:T(8,128)S(1)}, f32[8,128]{1,0:T(8,128)}, u32[]{:S(2)}) copy-start(f32[8,128]{1,0:T(8,128)} %decay_ref.3) | copy-start | bytes 12292
  39.6 42.1 %copy-start.10 = (f32[8,128]{1,0:T(8,128)S(1)}, f32[8,128]{1,0:T(8,128)}, u32[]{:S(2)}) copy-start(f32[8,128]{1,0:T(8,128)} %write_ref.3) | copy-start | bytes 12292
  45.9 74.7 %all-gather.6.cloned.1.call-start = ((), (), s32[]{:S(2)}) async-start(), calls=%async_computation.3 | async-start | bytes 1310720 | tf_op jit(solution)/shard_map/all_gather | solution.py:422
Sparse Core Ops, SparseCore 0:
  10.2 24.7 all-gather.3
  46.1 35.4 reduce-scatter.1
  83.4 25.1 all-gather.5

commit v2 on v1

--- a/solution.py
+++ b/solution.py
@@ -136,8 +136,9 @@
 
 
 def gdn_chain(
-    map_ref, mapt_ref, add_ref, pull_ref, mem_ref, grad_ref,
-    mem_in, mem_out, grad_in, grad_out, mem_send, mem_recv, grad_send, grad_recv,
+    map_ref, mapt_ref, add_ref, pull_ref, dkv_ref, mem_ref, grad_ref, adk_ref, adv_ref,
+    mem_in, mem_out, grad_in, grad_out, sums, groups,
+    mem_send, mem_recv, grad_send, grad_recv, sum_send, sum_recv, group_send, group_recv,
 ):
     n = lax.axis_size("ctx")
     me = lax.axis_index("ctx")
@@ -147,7 +148,12 @@
     barrier = pltpu.get_barrier_semaphore()
     for neighbour in (left, right):
         pl.semaphore_signal(barrier, inc=1, device_id=(neighbour, head_at), device_id_type=MESH)
-    pl.semaphore_wait(barrier, 2)
+    others = lax.axis_size("head")
+    for d in range(1, others):
+        pl.semaphore_signal(
+            barrier, inc=1, device_id=(me, lax.rem(head_at + d, others)), device_id_type=MESH
+        )
+    pl.semaphore_wait(barrier, 1 + others)
 
     def send(source, target, send_sem, recv_sem, head, to):
         return pltpu.make_async_remote_copy(
@@ -191,6 +197,38 @@
             grad_out[head] = mm(split(mapt_ref[head]), split(grad_in[head])) + pull_ref[head]
             copy.start()
 
+    def share(d):
+        return pltpu.make_async_remote_copy(
+            src_ref=groups.at[head_at],
+            dst_ref=groups.at[head_at],
+            send_sem=group_send.at[d],
+            recv_sem=group_recv.at[d],
+            device_id=(me, lax.rem(head_at + d, others)),
+            device_id_type=MESH,
+        )
+
+    def gather_sum(owner):
+        copy = send(sums, sums, sum_send, sum_recv, owner, left)
+
+        @pl.when(me == n - 1)
+        def _():
+            sums[owner] = dkv_ref[owner]
+
+        @pl.when(me < n - 1)
+        def _():
+            copy.wait_recv()
+            sums[owner] = sums[owner] + dkv_ref[owner]
+
+        @pl.when(owner < me)
+        def _():
+            copy.start()
+
+        @pl.when(owner == me)
+        def _():
+            groups[head_at] = sums[owner]
+            for d in range(1, others):
+                share(d).start()
+
     lag = jnp.clip((n - 1 - 2 * me) * 3, -heads, heads)
     mem_late, grad_late = jnp.maximum(-lag, 0), jnp.maximum(lag, 0)
 
@@ -205,9 +243,16 @@
         def _():
             retreat(grad_head)
 
+        sum_step = step - (n - 1 - me)
+        owner = lax.div(sum_step, 2)
+
+        @pl.when((sum_step >= 0) & (lax.rem(sum_step, 2) == 0) & (owner <= me))
+        def _():
+            gather_sum(owner)
+
         return carry
 
-    lax.fori_loop(0, 2 * heads, turn, 0)
+    lax.fori_loop(0, max(2 * heads, 3 * n), turn, 0)
 
     def drain(head, carry):
         @pl.when(me < n - 1)
@@ -221,6 +266,34 @@
         return carry
 
     lax.fori_loop(0, heads, drain, 0)
+
+    def drain_sums(owner, carry):
+        @pl.when(owner < me)
+        def _():
+            send(sums, sums, sum_send, sum_recv, owner, left).wait_send()
+
+        return carry
+
+    lax.fori_loop(0, n, drain_sums, 0)
+    for d in range(1, others):
+        here = lax.rem(head_at + others - d, others)
+        pltpu.make_async_remote_copy(
+            src_ref=groups.at[here],
+            dst_ref=groups.at[here],
+            send_sem=group_send.at[d],
+            recv_sem=group_recv.at[d],
+            device_id=(me, here),
+            device_id_type=MESH,
+        ).wait_recv()
+    each = others // KV_HEADS
+    for c in range(KV_HEADS):
+        total = groups[c * each]
+        for d in range(1, each):
+            total = total + groups[c * each + d]
+        adk_ref[:, c * HD : (c + 1) * HD] = total[:, :HD]
+        adv_ref[:, c * HD : (c + 1) * HD] = total[:, HD:]
+    for d in range(1, others):
+        share(d).wait_send()
     mem_ref[...] = mem_in[...]
     grad_ref[...] = grad_in[...]
 
@@ -303,60 +376,132 @@
     dwrite_ref[...] = scale_ref[...] * gate * (1.0 - gate) * dbeta
 
 
-def attention(lists_ref, q_ref, cot_ref, lse_ref, delta_ref, k_ref, v_ref, dq_ref, dkv_ref):
+def attention(lists_ref, q_ref, cot_ref, lse_ref, delta_ref, kv_ref, dq_ref, dkv_ref, q_all, cot_all):
     score_scale = HD ** (-0.5)
-    step = pl.program_id(0)
+    me = lax.axis_index("ctx")
     tokens = q_ref.shape[0]
     heads = q_ref.shape[1] // HD
-    keys = k_ref.shape[0]
     blocks_here = tokens // BLK
     n_blocks = lists_ref.shape[0] // (heads * TOPK)
-    first = lax.axis_index("ctx") * blocks_here
-
-    def stacked(ref):
-        return jnp.concatenate([ref[:, h * HD : (h + 1) * HD] for h in range(heads)], axis=0)
-
-    q, cot = stacked(q_ref), stacked(cot_ref)
-    k, v = k_ref[...], v_ref[...]
-    key_pos = step * keys + lax.broadcasted_iota(jnp.int32, (keys, tokens), 0)
-    key_block = key_pos // BLK
+    first = me * blocks_here
+    for h in range(heads):
+        q_all[h * tokens : (h + 1) * tokens, :] = q_ref[:, h * HD : (h + 1) * HD]
+        cot_all[h * tokens : (h + 1) * tokens, :] = cot_ref[:, h * HD : (h + 1) * HD]
+    dq_ref[...] = jnp.zeros_like(dq_ref)
     lane = lax.broadcasted_iota(jnp.int32, (1, tokens), 1)
-    row_pos = first * BLK + lane
+    row_pos = me * tokens + lane
     row_block = row_pos // BLK
-    own = (key_block == row_block) & (key_pos <= row_pos)
-    before = key_block < row_block
-    allowed = []
-    for h in range(heads):
-        member = None
-        for t in range(TOPK):
-            entry = jnp.zeros((1, tokens), jnp.int32)
-            for b in range(blocks_here):
-                listed = lists_ref[(h * n_blocks + first + b) * TOPK + t]
-                entry = jnp.where(lane // BLK == b, listed, entry)
-            hit = key_block == entry
-            member = hit if member is None else member | hit
-        allowed.append(own | (before & member))
-    scores = mm((k, None), (q, None), 1, 1)
-    dprobs = mm((v, None), (cot, None), 1, 1)
-    probs, dscores = [], []
-    for h in range(heads):
-        span = slice(h * tokens, (h + 1) * tokens)
-        mine = pl.ds(pl.multiple_of(first * BLK, tokens), tokens)
-        lse, delta = lse_ref[h : h + 1, mine], delta_ref[h : h + 1, mine]
-        prob = jnp.where(allowed[h], jnp.exp(scores[:, span] * score_scale - lse), 0.0)
-        probs.append(prob)
-        dscores.append(prob * (dprobs[:, span] - delta) * score_scale)
-    ds = split(jnp.concatenate(dscores, axis=1))
-    dkv_ref[:, :HD] = mm(ds, (q, None))
-    dkv_ref[:, HD:] = mm(split(jnp.concatenate(probs, axis=1)), (cot, None))
-    dq = mm(ds, (k, None), 0, 0)
-
-    @pl.when(step == 0)
-    def _():
-        dq_ref[...] = jnp.zeros_like(dq_ref)
-
-    for h in range(heads):
-        dq_ref[:, h * HD : (h + 1) * HD] += dq[h * tokens : (h + 1) * tokens]
+    mine = pl.ds(pl.multiple_of(me * tokens, tokens), tokens)
+
+    def block(owner):
+        q, cot = (q_all[...], None), (cot_all[...], None)
+        k, v = (kv_ref[owner][:, :HD], None), (kv_ref[owner][:, HD:], None)
+        key_pos = owner * tokens + lax.broadcasted_iota(jnp.int32, (tokens, tokens), 0)
+        key_block = key_pos // BLK
+        own = (key_block == row_block) & (key_pos <= row_pos)
+        before = key_block < row_block
+        scores = mm(k, q, 1, 1)
+        dprobs = mm(v, cot, 1, 1)
+        probs, dscores = [], []
+        for h in range(heads):
+            member = None
+            for t in range(TOPK):
+                entry = jnp.zeros((1, tokens), jnp.int32)
+                for b in range(blocks_here):
+                    listed = lists_ref[(h * n_blocks + first + b) * TOPK + t]
+                    entry = jnp.where(lane // BLK == b, listed, entry)
+                hit = key_block == entry
+                member = hit if member is None else member | hit
+            allowed = own | (before & member)
+            span = slice(h * tokens, (h + 1) * tokens)
+            lse, delta = lse_ref[h : h + 1, mine], delta_ref[h : h + 1, mine]
+            prob = jnp.where(allowed, jnp.exp(scores[:, span] * score_scale - lse), 0.0)
+            probs.append(prob)
+            dscores.append(prob * (dprobs[:, span] - delta) * score_scale)
+        ds = split(jnp.concatenate(dscores, axis=1))
+        dkv_ref[owner, :, :HD] = mm(ds, q)
+        dkv_ref[owner, :, HD:] = mm(split(jnp.concatenate(probs, axis=1)), cot)
+        dq = mm(ds, k, 0, 0)
+        for h in range(heads):
+            dq_ref[:, h * HD : (h + 1) * HD] += dq[h * tokens : (h + 1) * tokens]
+
+    return block
+
+
+def local_part(
+    lists_ref, aq_ref, acot_ref, lse_ref, delta_ref, ak_ref, av_ref,
+    q_ref, k_ref, v_ref, cot_ref, decay_ref, write_ref, rate_ref, scale_ref,
+    inv_ref, wu_ref, map_ref, mapt_ref, add_ref, pull_ref, gam_ref, beta_ref, dq_ref, dkv_ref,
+    kv, q_all, cot_all, far_send, far_recv, near_send, near_recv,
+):
+    n = lax.axis_size("ctx")
+    me, head_at = lax.axis_index("ctx"), lax.axis_index("head")
+    heads = aq_ref.shape[1] // HD
+    chips = n // 2
+    twin = me + 1 - 2 * lax.rem(me, 2)
+    barrier = pltpu.get_barrier_semaphore()
+    for d in range(1, n):
+        pl.semaphore_signal(
+            barrier, inc=1, device_id=(lax.rem(me + d, n), head_at), device_id_type=MESH
+        )
+    pl.semaphore_wait(barrier, n - 1)
+
+    group = head_at * heads // (Q_HEADS // KV_HEADS)
+    columns = pl.ds(pl.multiple_of(group * HD, HD), HD)
+    kv[me, :, :HD] = ak_ref[:, columns]
+    kv[me, :, HD:] = av_ref[:, columns]
+
+    def copy(slot, send_sem, recv_sem, index, to):
+        return pltpu.make_async_remote_copy(
+            src_ref=kv.at[slot],
+            dst_ref=kv.at[slot],
+            send_sem=send_sem.at[index],
+            recv_sem=recv_sem.at[index],
+            device_id=(to, head_at),
+            device_id_type=MESH,
+        )
+
+    def source(d):
+        return lax.rem(me + n - 2 * d, n)
+
+    def far(d):
+        return copy(me, far_send, far_recv, d, lax.rem(me + 2 * d, n))
+
+    for d in range(1, chips):
+        far(d).start()
+    copy(me, near_send, near_recv, 0, twin).start()
+
+    gdn_local(
+        q_ref, k_ref, v_ref, cot_ref, decay_ref, write_ref, rate_ref, scale_ref,
+        inv_ref, wu_ref, map_ref, mapt_ref, add_ref, pull_ref, gam_ref, beta_ref,
+    )
+    block = attention(
+        lists_ref, aq_ref, acot_ref, lse_ref, delta_ref, kv, dq_ref, dkv_ref, q_all, cot_all
+    )
+    for d in range(1, chips):
+        copy(source(d), far_send, far_recv, d, twin).wait_recv()
+        copy(source(d), near_send, near_recv, d, twin).start()
+
+    def visit(start):
+        def turn(d, carry):
+            owner = lax.rem(start + n - 2 * d, n)
+
+            @pl.when(owner <= me)
+            def _():
+                block(owner)
+
+            return carry
+
+        lax.fori_loop(0, chips, turn, 0)
+
+    visit(me)
+    for d in range(chips):
+        copy(lax.rem(twin + n - 2 * d, n), near_send, near_recv, d, twin).wait_recv()
+    visit(twin)
+    for d in range(1, chips):
+        far(d).wait_send()
+    for d in range(chips):
+        copy(source(d), near_send, near_recv, d, twin).wait_send()
 
 
 def on_device(
@@ -367,76 +512,59 @@
     local_heads = attn_q.shape[1] // HD
     ctx = lax.axis_size("ctx")
     head_devices = lax.axis_size("head")
-    n_rows = tokens * ctx
-    kv_group = lax.axis_index("head") * local_heads // (Q_HEADS // KV_HEADS)
-    own_kv = jnp.concatenate(
-        [
-            lax.dynamic_slice_in_dim(attn_k, kv_group * HD, HD, 1),
-            lax.dynamic_slice_in_dim(attn_v, kv_group * HD, HD, 1),
-        ],
-        axis=1,
-    )
-    all_kv = lax.all_gather(own_kv, "ctx", axis=0, tiled=True)
-
     value_heads = gdn_v.shape[1] // GDIM
     rates, scales = decay_rate[:, None], write_scale[:, None]
     vmem = pl.BlockSpec(memory_space=pltpu.VMEM)
     square = jax.ShapeDtypeStruct((value_heads, GDIM, GDIM), F32)
     gates = jax.ShapeDtypeStruct((value_heads, tokens), F32)
-    inverse, wu, maps, maps_t, adds, pulls, gam, beta = pl.pallas_call(
-        gdn_local,
+    sums = (ctx, tokens, 2 * HD)
+    far, near = pltpu.SemaphoreType.DMA((ctx // 2,)), pltpu.SemaphoreType.DMA((ctx // 2,))
+    inverse, wu, maps, maps_t, adds, pulls, gam, beta, grad_q, dkv = pl.pallas_call(
+        local_part,
         out_shape=(
             jax.ShapeDtypeStruct((value_heads, tokens, tokens), F32),
             jax.ShapeDtypeStruct((value_heads, tokens, 2 * GDIM), F32),
             square, square, square, square, gates, gates,
+            jax.ShapeDtypeStruct((tokens, local_heads * HD), F32),
+            jax.ShapeDtypeStruct(sums, F32),
         ),
-        in_specs=[vmem] * 8,
-        out_specs=[vmem] * 8,
-        compiler_params=pltpu.CompilerParams(vmem_limit_bytes=VMEM_BYTES),
-        name="gdn_local",
-    )(gdn_q, gdn_k, gdn_v, gdn_cot, decay_logit, write_logit, rates, scales)
-
-    keys = min(256, n_rows)
-    grad_q, dkv = pl.pallas_call(
-        attention,
-        grid=(n_rows // keys,),
-        out_shape=(
-            jax.ShapeDtypeStruct((tokens, local_heads * HD), F32),
-            jax.ShapeDtypeStruct((n_rows, 2 * HD), F32),
-        ),
-        in_specs=[
-            pl.BlockSpec(memory_space=pltpu.SMEM),
-            vmem, vmem, vmem, vmem,
-            pl.BlockSpec((keys, HD), lambda i: (i, 0)),
-            pl.BlockSpec((keys, HD), lambda i: (i, 1)),
+        in_specs=[pl.BlockSpec(memory_space=pltpu.SMEM)] + [vmem] * 14,
+        out_specs=[vmem] * 10,
+        scratch_shapes=[
+            pltpu.VMEM(sums, BF16),
+            pltpu.VMEM((local_heads * tokens, HD), BF16),
+            pltpu.VMEM((local_heads * tokens, HD), BF16),
+            far, far, near, near,
         ],
-        out_specs=(
-            pl.BlockSpec((tokens, local_heads * HD), lambda i: (0, 0)),
-            pl.BlockSpec((keys, 2 * HD), lambda i: (i, 0)),
-        ),
-        compiler_params=pltpu.CompilerParams(vmem_limit_bytes=VMEM_BYTES),
-        name="attention",
-    )(block_lists.reshape(-1), attn_q, attn_cot, attn_lse, attn_delta, all_kv, all_kv)
-
-    mine = lax.psum_scatter(dkv, "ctx", scatter_dimension=0, tiled=True)
-    groups = lax.all_gather(mine, "head", axis=0)
-    groups = groups.reshape(KV_HEADS, head_devices // KV_HEADS, tokens, 2 * HD).sum(axis=1)
-    attn_dk = jnp.concatenate([groups[c, :, :HD] for c in range(KV_HEADS)], axis=1)
-    attn_dv = jnp.concatenate([groups[c, :, HD:] for c in range(KV_HEADS)], axis=1)
-
-    buffer = pltpu.VMEM((value_heads, GDIM, GDIM), F32)
-    sems = pltpu.SemaphoreType.DMA((value_heads,))
-    mem, grad = pl.pallas_call(
-        gdn_chain,
-        out_shape=(square, square),
-        in_specs=[vmem] * 4,
-        out_specs=(vmem, vmem),
-        scratch_shapes=[buffer] * 4 + [sems] * 4,
         compiler_params=pltpu.CompilerParams(
             collective_id=0, has_side_effects=True, vmem_limit_bytes=VMEM_BYTES
         ),
+        name="local_part",
+    )(
+        block_lists.reshape(-1), attn_q, attn_cot, attn_lse, attn_delta, attn_k, attn_v,
+        gdn_q, gdn_k, gdn_v, gdn_cot, decay_logit, write_logit, rates, scales,
+    )
+
+    buffer = pltpu.VMEM((value_heads, GDIM, GDIM), F32)
+    sems = pltpu.SemaphoreType.DMA((value_heads,))
+    sum_sems = pltpu.SemaphoreType.DMA((ctx,))
+    head_sems = pltpu.SemaphoreType.DMA((head_devices,))
+    key_grads = jax.ShapeDtypeStruct((tokens, KV_HEADS * HD), F32)
+    mem, grad, attn_dk, attn_dv = pl.pallas_call(
+        gdn_chain,
+        out_shape=(square, square, key_grads, key_grads),
+        in_specs=[vmem] * 5,
+        out_specs=[vmem] * 4,
+        scratch_shapes=[buffer] * 4
+        + [pltpu.VMEM(sums, F32), pltpu.VMEM((head_devices, tokens, 2 * HD), F32)]
+        + [sems] * 4
+        + [sum_sems] * 2
+        + [head_sems] * 2,
+        compiler_params=pltpu.CompilerParams(
+            collective_id=1, has_side_effects=True, vmem_limit_bytes=VMEM_BYTES
+        ),
         name="gdn_chain",
-    )(maps, maps_t, adds, pulls)
+    )(maps, maps_t, adds, pulls, dkv)
 
     dq, dk, dv, ddecay, dwrite = pl.pallas_call(
         gdn_grads,

time: 131 us -> 104 us (0.79)
  the two profiles are of different devices: /device:TPU:0 before, /device:TPU:25 now
where the time goes in v2:
time: 104 us; the launch traced here: 103 us
  Pallas kernels  86.3 us (83%)
  local copies, waits for them, and re-layouts  16.4 us (16%)
    pallas_call x1, Pallas kernels, on_device(): pl.pallas_call(gdn_chain, out_shape=(square, square, key_grads, key_grads...  56.2 us
    pallas_call x1, Pallas kernels, on_device(): pl.pallas_call(local_part, out_shape=(jax.ShapeDtypeStruct((value_heads,...  23.4 us
    unnamed x36, local copies, waits for them, and re-layouts  14.8 us
    pallas_call x1, Pallas kernels, on_device(): pl.pallas_call(gdn_grads, out_shape=(jax.ShapeDtypeStruct(gdn_q.shape, F3...  6.74 us

profile of v2, /device:TPU:25, one launch (start us, length us, event | category | flops | bytes accessed | tf_op | source)
XLA Modules:
  0.0 103.4 jit_solution(7315138673015535497)
XLA Ops:
  0.6 0.7 copy.28.rate_ref
  1.4 0.7 copy.29.scale_ref
  2.1 0.8 copy.27
  2.9 0.1 reshape.19.lists_ref
  3.0 0.0 copy-start.1
  3.0 0.9 copy-done.1
  3.9 0.9 copy-done.3
  4.9 0.9 copy-done.5
  5.8 0.9 copy-done.6
  6.7 0.9 copy-done.7
  7.7 0.9 copy-done.8
  8.6 0.9 copy-done.9
  9.5 0.9 copy-done.10
  10.4 0.7 copy-done.11
  11.1 0.7 copy-done.12
  11.9 0.7 copy-done.13
  12.5 0.7 copy-done.14
  13.2 23.4 %local_part.1 = (f32[8,128,128]{2,1,0:T(8,128)S(1)}, f32[8,128,256]{2,1,0:T(8,128)S(1)}, f32[8,128,128]{2,1,0:T(8,128)S(1)}, f32[8,128,128]{2,1,0:T(8,128)S(1)},...) custom-call(s32[256]{0:T(256)S(1)} %reshape.19.lists_ref, ...), custom_call_target="tpu_custom_call" | custom-call | tf_op jit(solution)/shard_map/local_part/pallas_call | solution.py:522
  36.7 1.6 %copy-done = f32[8,128,512]{2,1,0:T(8,128)S(1)} copy-done((f32[8,128,512]{2,1,0:T(8,128)S(1)}, f32[8,128,512]{2,1,0:T(8,128)}, u32[]{:S(2)}) %copy-start) | copy-done | bytes 2097176
  38.2 56.2 %gdn_chain.1 = (f32[8,128,128]{2,1,0:T(8,128)S(1)}, f32[8,128,128]{2,1,0:T(8,128)S(1)}, f32[128,512]{1,0:T(8,128)S(1)}, f32[128,512]{1,0:T(8,128)S(1)}) custom-call(f32[8,128,128]{2,1,0:T(8,128)S(1)} %get-tuple-element.28.map_ref, f32[8,128,128]{2,1,0:T(8,128)S(1)} %get-tuple-element.29.mapt_ref, f32[8,128,128]{2,1,0:T(8,128)S(1)} %get-tuple-element.30.add_ref, ...), custom_call_target="tpu_custom_call" | custom-call | tf_op jit(solution)/shard_map/gdn_chain/pallas_call | solution.py:553
  94.5 6.7 %gdn_grads.1 = (f32[128,512]{1,0:T(8,128)}, f32[128,512]{1,0:T(8,128)}, f32[128,1024]{1,0:T(8,128)}, f32[8,128]{1,0:T(8,128)}, f32[8,128]{1,0:T(8,128)}) custom-call(bf16[128,512]{1,0:T(8,128)(2,1)S(1)} %copy-done.5, bf16[128,512]{1,0:T(8,128)(2,1)S(1)} %copy-done.6, bf16[128,1024]{1,0:T(8,128)(2,1)S(1)} %copy-done.2, bf16[128,1024]{1,0:T(8,128)(2,1)S(1)} %copy-done.4, ...), custom_call_target="tpu_custom_call" | custom-call | tf_op jit(solution)/shard_map/gdn_grads/pallas_call | solution.py:569
  101.2 0.8 copy.35
  102.0 0.7 copy.36
  102.7 0.7 copy.37
  (18 shorter events, 0.0 us)
Async XLA Ops:
  3.0 1.0 copy-start.1
  3.9 0.9 copy-start.3
  4.9 0.9 copy-start.5
  5.8 0.9 copy-start.6
  6.7 0.9 copy-start.7
  7.7 0.9 copy-start.8
  8.6 0.9 copy-start.9
  9.5 0.9 copy-start.10
  10.4 0.7 copy-start.11
  11.1 0.7 copy-start.12
  11.9 0.7 copy-start.13
  12.5 0.7 copy-start.14
  36.6 1.6 %copy-start = (f32[8,128,512]{2,1,0:T(8,128)S(1)}, f32[8,128,512]{2,1,0:T(8,128)}, u32[]{:S(2)}) copy-start(f32[8,128,512]{2,1,0:T(8,128)} %get-tuple-element.32.dkv_ref) | copy-start | bytes 6291460
  38.2 56.2 %copy-start.2 = (bf16[128,1024]{1,0:T(8,128)(2,1)S(1)}, bf16[128,1024]{1,0:T(8,128)(2,1)}, u32[]{:S(2)}) copy-start(bf16[128,1024]{1,0:T(8,128)(2,1)} %v_ref.3) | copy-start | bytes 786436
  38.2 56.2 %copy-start.4 = (bf16[128,1024]{1,0:T(8,128)(2,1)S(1)}, bf16[128,1024]{1,0:T(8,128)(2,1)}, u32[]{:S(2)}) copy-start(bf16[128,1024]{1,0:T(8,128)(2,1)} %cot_ref.3) | copy-start | bytes 786436
  38.2 56.2 %copy-start.15 = (f32[8,128]{1,0:T(8,128)S(1)}, f32[8,128]{1,0:T(8,128)}, u32[]{:S(2)}) copy-start(f32[8,128]{1,0:T(8,128)} %write_ref.3) | copy-start | bytes 12292

commit v3 on v2

--- a/solution.py
+++ b/solution.py
@@ -13,7 +13,7 @@
 TOPK = 4
 F32 = jnp.float32
 BF16 = jnp.bfloat16
-VMEM_BYTES = 48 * 1024 * 1024
+VMEM_BYTES = 58 * 1024 * 1024
 MESH = pl.DeviceIdType.MESH
 
 
@@ -68,6 +68,11 @@
     return ref[:, head * GDIM : (head + 1) * GDIM]
 
 
+def per_head(ref, like):
+    heads, width = like.shape
+    return jnp.concatenate([jnp.full((1, width), ref[v], F32) for v in range(heads)], axis=0)
+
+
 def triangles(size):
     rows = lax.broadcasted_iota(jnp.int32, (size, size), 0)
     cols = lax.broadcasted_iota(jnp.int32, (size, size), 1)
@@ -82,8 +87,8 @@
     key_heads = q_ref.shape[1] // GDIM
     value_heads = v_ref.shape[1] // GDIM
     ratio = value_heads // key_heads
-    gam = lane_cumsum(-rate_ref[...] * softplus(decay_ref[...]), False)
-    beta = scale_ref[...] * sigmoid(write_ref[...])
+    gam = lane_cumsum(-per_head(rate_ref, decay_ref) * softplus(decay_ref[...]), False)
+    beta = per_head(scale_ref, write_ref) * sigmoid(write_ref[...])
     gam_ref[...] = gam
     beta_ref[...] = beta
     rows, cols = triangles(size)
@@ -133,169 +138,6 @@
             add_ref[v] = ends[:, GDIM:]
             reads = now * qn - mm(split(upto[n] * cross), split(wu[:, :GDIM]))
             pull_ref[v] = mm(split(reads.T), split(head_cols(cot_ref, v)))
-
-
-def gdn_chain(
-    map_ref, mapt_ref, add_ref, pull_ref, dkv_ref, mem_ref, grad_ref, adk_ref, adv_ref,
-    mem_in, mem_out, grad_in, grad_out, sums, groups,
-    mem_send, mem_recv, grad_send, grad_recv, sum_send, sum_recv, group_send, group_recv,
-):
-    n = lax.axis_size("ctx")
-    me = lax.axis_index("ctx")
-    head_at = lax.axis_index("head")
-    heads = map_ref.shape[0]
-    right, left = lax.rem(me + 1, n), lax.rem(me + n - 1, n)
-    barrier = pltpu.get_barrier_semaphore()
-    for neighbour in (left, right):
-        pl.semaphore_signal(barrier, inc=1, device_id=(neighbour, head_at), device_id_type=MESH)
-    others = lax.axis_size("head")
-    for d in range(1, others):
-        pl.semaphore_signal(
-            barrier, inc=1, device_id=(me, lax.rem(head_at + d, others)), device_id_type=MESH
-        )
-    pl.semaphore_wait(barrier, 1 + others)
-
-    def send(source, target, send_sem, recv_sem, head, to):
-        return pltpu.make_async_remote_copy(
-            src_ref=source.at[head],
-            dst_ref=target.at[head],
-            send_sem=send_sem.at[head],
-            recv_sem=recv_sem.at[head],
-            device_id=(to, head_at),
-            device_id_type=MESH,
-        )
-
-    def advance(head):
-        copy = send(mem_out, mem_in, mem_send, mem_recv, head, right)
-
-        @pl.when(me == 0)
-        def _():
-            mem_in[head] = jnp.zeros((GDIM, GDIM), F32)
-
-        @pl.when(me > 0)
-        def _():
-            copy.wait_recv()
-
-        @pl.when(me < n - 1)
-        def _():
-            mem_out[head] = mm(split(map_ref[head]), split(mem_in[head])) + add_ref[head]
-            copy.start()
-
-    def retreat(head):
-        copy = send(grad_out, grad_in, grad_send, grad_recv, head, left)
-
-        @pl.when(me == n - 1)
-        def _():
-            grad_in[head] = jnp.zeros((GDIM, GDIM), F32)
-
-        @pl.when(me < n - 1)
-        def _():
-            copy.wait_recv()
-
-        @pl.when(me > 0)
-        def _():
-            grad_out[head] = mm(split(mapt_ref[head]), split(grad_in[head])) + pull_ref[head]
-            copy.start()
-
-    def share(d):
-        return pltpu.make_async_remote_copy(
-            src_ref=groups.at[head_at],
-            dst_ref=groups.at[head_at],
-            send_sem=group_send.at[d],
-            recv_sem=group_recv.at[d],
-            device_id=(me, lax.rem(head_at + d, others)),
-            device_id_type=MESH,
-        )
-
-    def gather_sum(owner):
-        copy = send(sums, sums, sum_send, sum_recv, owner, left)
-
-        @pl.when(me == n - 1)
-        def _():
-            sums[owner] = dkv_ref[owner]
-
-        @pl.when(me < n - 1)
-        def _():
-            copy.wait_recv()
-            sums[owner] = sums[owner] + dkv_ref[owner]
-
-        @pl.when(owner < me)
-        def _():
-            copy.start()
-
-        @pl.when(owner == me)
-        def _():
-            groups[head_at] = sums[owner]
-            for d in range(1, others):
-                share(d).start()
-
-    lag = jnp.clip((n - 1 - 2 * me) * 3, -heads, heads)
-    mem_late, grad_late = jnp.maximum(-lag, 0), jnp.maximum(lag, 0)
-
-    def turn(step, carry):
-        mem_head, grad_head = step - mem_late, step - grad_late
-
-        @pl.when((mem_head >= 0) & (mem_head < heads))
-        def _():
-            advance(mem_head)
-
-        @pl.when((grad_head >= 0) & (grad_head < heads))
-        def _():
-            retreat(grad_head)
-
-        sum_step = step - (n - 1 - me)
-        owner = lax.div(sum_step, 2)
-
-        @pl.when((sum_step >= 0) & (lax.rem(sum_step, 2) == 0) & (owner <= me))
-        def _():
-            gather_sum(owner)
-
-        return carry
-
-    lax.fori_loop(0, max(2 * heads, 3 * n), turn, 0)
-
-    def drain(head, carry):
-        @pl.when(me < n - 1)
-        def _():
-            send(mem_out, mem_in, mem_send, mem_recv, head, right).wait_send()
-
-        @pl.when(me > 0)
-        def _():
-            send(grad_out, grad_in, grad_send, grad_recv, head, left).wait_send()
-
-        return carry
-
-    lax.fori_loop(0, heads, drain, 0)
-
-    def drain_sums(owner, carry):
-        @pl.when(owner < me)
-        def _():
-            send(sums, sums, sum_send, sum_recv, owner, left).wait_send()
-
-        return carry
-
-    lax.fori_loop(0, n, drain_sums, 0)
-    for d in range(1, others):
-        here = lax.rem(head_at + others - d, others)
-        pltpu.make_async_remote_copy(
-            src_ref=groups.at[here],
-            dst_ref=groups.at[here],
-            send_sem=group_send.at[d],
-            recv_sem=group_recv.at[d],
-            device_id=(me, here),
-            device_id_type=MESH,
-        ).wait_recv()
-    each = others // KV_HEADS
-    for c in range(KV_HEADS):
-        total = groups[c * each]
-        for d in range(1, each):
-            total = total + groups[c * each + d]
-        adk_ref[:, c * HD : (c + 1) * HD] = total[:, :HD]
-        adv_ref[:, c * HD : (c + 1) * HD] = total[:, HD:]
-    for d in range(1, others):
-        share(d).wait_send()
-    mem_ref[...] = mem_in[...]
-    grad_ref[...] = grad_in[...]
 
 
 def gdn_grads(
@@ -371,9 +213,9 @@
             ends.append(jnp.sum(jnp.sum(both, axis=0, keepdims=True), axis=1, keepdims=True))
     dlog = lane_cumsum(jnp.concatenate(dgam_rows, axis=0), True) + jnp.concatenate(ends, axis=0)
     dbeta = jnp.concatenate(dbeta_rows, axis=0)
-    ddecay_ref[...] = -rate_ref[...] * sigmoid(decay_ref[...]) * dlog
+    ddecay_ref[...] = -per_head(rate_ref, decay_ref) * sigmoid(decay_ref[...]) * dlog
     gate = sigmoid(write_ref[...])
-    dwrite_ref[...] = scale_ref[...] * gate * (1.0 - gate) * dbeta
+    dwrite_ref[...] = per_head(scale_ref, write_ref) * gate * (1.0 - gate) * dbeta
 
 
 def attention(lists_ref, q_ref, cot_ref, lse_ref, delta_ref, kv_ref, dq_ref, dkv_ref, q_all, cot_all):
@@ -382,7 +224,6 @@
     tokens = q_ref.shape[0]
     heads = q_ref.shape[1] // HD
     blocks_here = tokens // BLK
-    n_blocks = lists_ref.shape[0] // (heads * TOPK)
     first = me * blocks_here
     for h in range(heads):
         q_all[h * tokens : (h + 1) * tokens, :] = q_ref[:, h * HD : (h + 1) * HD]
@@ -408,7 +249,7 @@
             for t in range(TOPK):
                 entry = jnp.zeros((1, tokens), jnp.int32)
                 for b in range(blocks_here):
-                    listed = lists_ref[(h * n_blocks + first + b) * TOPK + t]
+                    listed = lists_ref[h, first + b, t]
                     entry = jnp.where(lane // BLK == b, listed, entry)
                 hit = key_block == entry
                 member = hit if member is None else member | hit
@@ -428,23 +269,48 @@
     return block
 
 
-def local_part(
-    lists_ref, aq_ref, acot_ref, lse_ref, delta_ref, ak_ref, av_ref,
-    q_ref, k_ref, v_ref, cot_ref, decay_ref, write_ref, rate_ref, scale_ref,
-    inv_ref, wu_ref, map_ref, mapt_ref, add_ref, pull_ref, gam_ref, beta_ref, dq_ref, dkv_ref,
-    kv, q_all, cot_all, far_send, far_recv, near_send, near_recv,
+def through_chain(
+    lists_ref, aq_hbm, acot_hbm, lse_hbm, delta_hbm, ak_hbm, av_hbm,
+    q_hbm, k_hbm, v_hbm, cot_hbm, decay_hbm, write_hbm, rate_ref, scale_ref,
+    inv_ref, wu_ref, gam_ref, beta_ref, dq_ref, mem_ref, grad_ref, adk_ref, adv_ref,
+    q_ref, k_ref, v_ref, cot_ref, decay_ref, write_ref,
+    aq_ref, acot_ref, lse_ref, delta_ref, ak_ref, av_ref, load_sem,
+    map_ref, mapt_ref, add_ref, pull_ref, kv, q_all, cot_all, dkv, twin_in, far_in, groups,
+    mem_out, grad_out, far_send, far_recv, near_send, near_recv,
+    mem_send, mem_recv, grad_send, grad_recv, pair_send, pair_recv, sum_send, sum_recv,
+    group_send, group_recv,
 ):
     n = lax.axis_size("ctx")
     me, head_at = lax.axis_index("ctx"), lax.axis_index("head")
     heads = aq_ref.shape[1] // HD
     chips = n // 2
+    loads = [
+        pltpu.make_async_copy(source, target, load_sem.at[i])
+        for i, (source, target) in enumerate(
+            (
+                (ak_hbm, ak_ref), (av_hbm, av_ref),
+                (q_hbm, q_ref), (k_hbm, k_ref), (v_hbm, v_ref), (cot_hbm, cot_ref),
+                (decay_hbm, decay_ref), (write_hbm, write_ref),
+                (aq_hbm, aq_ref), (acot_hbm, acot_ref), (lse_hbm, lse_ref), (delta_hbm, delta_ref),
+            )
+        )
+    ]
+    for load in loads:
+        load.start()
     twin = me + 1 - 2 * lax.rem(me, 2)
     barrier = pltpu.get_barrier_semaphore()
     for d in range(1, n):
         pl.semaphore_signal(
             barrier, inc=1, device_id=(lax.rem(me + d, n), head_at), device_id_type=MESH
         )
-    pl.semaphore_wait(barrier, n - 1)
+    others = lax.axis_size("head")
+    for d in range(1, others):
+        pl.semaphore_signal(
+            barrier, inc=1, device_id=(me, lax.rem(head_at + d, others)), device_id_type=MESH
+        )
+    for load in loads[:2]:
+        load.wait()
+    pl.semaphore_wait(barrier, n + others - 2)
 
     group = head_at * heads // (Q_HEADS // KV_HEADS)
     columns = pl.ds(pl.multiple_of(group * HD, HD), HD)
@@ -470,34 +336,222 @@
     for d in range(1, chips):
         far(d).start()
     copy(me, near_send, near_recv, 0, twin).start()
+    for load in loads[2:8]:
+        load.wait()
 
     gdn_local(
         q_ref, k_ref, v_ref, cot_ref, decay_ref, write_ref, rate_ref, scale_ref,
         inv_ref, wu_ref, map_ref, mapt_ref, add_ref, pull_ref, gam_ref, beta_ref,
     )
+    for load in loads[8:]:
+        load.wait()
     block = attention(
-        lists_ref, aq_ref, acot_ref, lse_ref, delta_ref, kv, dq_ref, dkv_ref, q_all, cot_all
+        lists_ref, aq_ref, acot_ref, lse_ref, delta_ref, kv, dq_ref, dkv, q_all, cot_all
     )
     for d in range(1, chips):
         copy(source(d), far_send, far_recv, d, twin).wait_recv()
         copy(source(d), near_send, near_recv, d, twin).start()
 
-    def visit(start):
-        def turn(d, carry):
-            owner = lax.rem(start + n - 2 * d, n)
+    chip, core = lax.div(me, 2), lax.rem(me, 2)
+
+    def pair(c):
+        return pltpu.make_async_remote_copy(
+            src_ref=dkv.at[2 * c + 1 - core],
+            dst_ref=twin_in.at[c],
+            send_sem=pair_send.at[c],
+            recv_sem=pair_recv.at[c],
+            device_id=(twin, head_at),
+            device_id_type=MESH,
+        )
+
+    def down(c):
+        return pltpu.make_async_remote_copy(
+            src_ref=dkv.at[2 * c + core],
+            dst_ref=far_in.at[chip - c],
+            send_sem=sum_send.at[chip - c],
+            recv_sem=sum_recv.at[chip - c],
+            device_id=(2 * c + core, head_at),
+            device_id_type=MESH,
+        )
+
+    def visit(start, to_twin):
+        def turn(c, carry):
+            owner = 2 * c + lax.rem(start, 2)
 
             @pl.when(owner <= me)
             def _():
                 block(owner)
+                if to_twin:
+                    pair(c).start()
 
             return carry
 
         lax.fori_loop(0, chips, turn, 0)
 
-    visit(me)
+    visit(me, False)
     for d in range(chips):
         copy(lax.rem(twin + n - 2 * d, n), near_send, near_recv, d, twin).wait_recv()
-    visit(twin)
+    visit(twin, True)
+
+    def combine(c, carry):
+        @pl.when(2 * c + core <= twin)
+        def _():
+            pair(c).wait_recv()
+            dkv[2 * c + core] = dkv[2 * c + core] + twin_in[c]
+
+        @pl.when(c < chip)
+        def _():
+            down(c).start()
+
+        return carry
+
+    lax.fori_loop(0, chips, combine, 0)
+
+    def share(d):
+        return pltpu.make_async_remote_copy(
+            src_ref=groups.at[head_at],
+            dst_ref=groups.at[head_at],
+            send_sem=group_send.at[d],
+            recv_sem=group_recv.at[d],
+            device_id=(me, lax.rem(head_at + d, others)),
+            device_id_type=MESH,
+        )
+
+    def finish_sum():
+        groups[head_at] = dkv[me]
+
+        def turn(d, carry):
+            @pl.when(chip + d < chips)
+            def _():
+                pltpu.make_async_remote_copy(
+                    src_ref=dkv.at[me],
+                    dst_ref=far_in.at[d],
+                    send_sem=sum_send.at[d],
+                    recv_sem=sum_recv.at[d],
+                    device_id=(twin, head_at),
+                    device_id_type=MESH,
+                ).wait_recv()
+                groups[head_at] = groups[head_at] + far_in[d]
+
+            return carry
+
+        lax.fori_loop(1, chips, turn, 0)
+        for d in range(1, others):
+            share(d).start()
+
+    right, left = lax.rem(me + 1, n), lax.rem(me + n - 1, n)
+    value_heads = map_ref.shape[0]
+
+    def send(source, target, send_sem, recv_sem, head, to):
+        return pltpu.make_async_remote_copy(
+            src_ref=source.at[head],
+            dst_ref=target.at[head],
+            send_sem=send_sem.at[head],
+            recv_sem=recv_sem.at[head],
+            device_id=(to, head_at),
+            device_id_type=MESH,
+        )
+
+    def advance(head):
+        copy = send(mem_out, mem_ref, mem_send, mem_recv, head, right)
+
+        @pl.when(me == 0)
+        def _():
+            mem_ref[head] = jnp.zeros((GDIM, GDIM), F32)
+
+        @pl.when(me > 0)
+        def _():
+            copy.wait_recv()
+
+        @pl.when(me < n - 1)
+        def _():
+            mem_out[head] = mm(split(map_ref[head]), split(mem_ref[head])) + add_ref[head]
+            copy.start()
+
+    def retreat(head):
+        copy = send(grad_out, grad_ref, grad_send, grad_recv, head, left)
+
+        @pl.when(me == n - 1)
+        def _():
+            grad_ref[head] = jnp.zeros((GDIM, GDIM), F32)
+
+        @pl.when(me < n - 1)
+        def _():
+            copy.wait_recv()
+
+        @pl.when(me > 0)
+        def _():
+            grad_out[head] = mm(split(mapt_ref[head]), split(grad_ref[head])) + pull_ref[head]
+            copy.start()
+
+    steps = 2 * value_heads
+    sum_at = jnp.minimum((chips - 1 - chip) * 5, steps - 1)
+    lag = jnp.clip((n - 1 - 2 * me) * 3, -value_heads, value_heads)
+    mem_late, grad_late = jnp.maximum(-lag, 0), jnp.maximum(lag, 0)
+
+    def turn(step, carry):
+        mem_head, grad_head = step - mem_late, step - grad_late
+
+        @pl.when((mem_head >= 0) & (mem_head < value_heads))
+        def _():
+            advance(mem_head)
+
+        @pl.when((grad_head >= 0) & (grad_head < value_heads))
+        def _():
+            retreat(grad_head)
+
+        @pl.when(step == sum_at)
+        def _():
+            finish_sum()
+
+        return carry
+
+    lax.fori_loop(0, steps, turn, 0)
+
+    def drain(head, carry):
+        @pl.when(me < n - 1)
+        def _():
+            send(mem_out, mem_ref, mem_send, mem_recv, head, right).wait_send()
+
+        @pl.when(me > 0)
+        def _():
+            send(grad_out, grad_ref, grad_send, grad_recv, head, left).wait_send()
+
+        return carry
+
+    lax.fori_loop(0, value_heads, drain, 0)
+
+    def drain_sums(c, carry):
+        @pl.when(2 * c + 1 - core <= me)
+        def _():
+            pair(c).wait_send()
+
+        @pl.when(c < chip)
+        def _():
+            down(c).wait_send()
+
+        return carry
+
+    lax.fori_loop(0, chips, drain_sums, 0)
+    for d in range(1, others):
+        here = lax.rem(head_at + others - d, others)
+        pltpu.make_async_remote_copy(
+            src_ref=groups.at[here],
+            dst_ref=groups.at[here],
+            send_sem=group_send.at[d],
+            recv_sem=group_recv.at[d],
+            device_id=(me, here),
+            device_id_type=MESH,
+        ).wait_recv()
+    each = others // KV_HEADS
+    for c in range(KV_HEADS):
+        total = groups[c * each]
+        for d in range(1, each):
+            total = total + groups[c * each + d]
+        adk_ref[:, c * HD : (c + 1) * HD] = total[:, :HD]
+        adv_ref[:, c * HD : (c + 1) * HD] = total[:, HD:]
+    for d in range(1, others):
+        share(d).wait_send()
     for d in range(1, chips):
         far(d).wait_send()
     for d in range(chips):
@@ -513,58 +567,49 @@
     ctx = lax.axis_size("ctx")
     head_devices = lax.axis_size("head")
     value_heads = gdn_v.shape[1] // GDIM
-    rates, scales = decay_rate[:, None], write_scale[:, None]
-    vmem = pl.BlockSpec(memory_space=pltpu.VMEM)
+    vmem, smem = (pl.BlockSpec(memory_space=space) for space in (pltpu.VMEM, pltpu.SMEM))
+
     square = jax.ShapeDtypeStruct((value_heads, GDIM, GDIM), F32)
     gates = jax.ShapeDtypeStruct((value_heads, tokens), F32)
-    sums = (ctx, tokens, 2 * HD)
-    far, near = pltpu.SemaphoreType.DMA((ctx // 2,)), pltpu.SemaphoreType.DMA((ctx // 2,))
-    inverse, wu, maps, maps_t, adds, pulls, gam, beta, grad_q, dkv = pl.pallas_call(
-        local_part,
+    key_grads = jax.ShapeDtypeStruct((tokens, KV_HEADS * HD), F32)
+    buffer = pltpu.VMEM((value_heads, GDIM, GDIM), F32)
+    stacked = pltpu.VMEM((local_heads * tokens, HD), BF16)
+
+    def sums(count, kind):
+        return pltpu.VMEM((count, tokens, 2 * HD), kind)
+
+    def sems(count):
+        return pltpu.SemaphoreType.DMA((count,))
+
+    attn_in = (attn_q, attn_cot, attn_lse, attn_delta, attn_k, attn_v)
+    gdn_in = (gdn_q, gdn_k, gdn_v, gdn_cot, decay_logit, write_logit)
+    chips = ctx // 2
+    hbm = pl.BlockSpec(memory_space=pltpu.HBM)
+    inverse, wu, gam, beta, grad_q, mem, grad, attn_dk, attn_dv = pl.pallas_call(
+        through_chain,
         out_shape=(
             jax.ShapeDtypeStruct((value_heads, tokens, tokens), F32),
             jax.ShapeDtypeStruct((value_heads, tokens, 2 * GDIM), F32),
-            square, square, square, square, gates, gates,
+            gates, gates,
             jax.ShapeDtypeStruct((tokens, local_heads * HD), F32),
-            jax.ShapeDtypeStruct(sums, F32),
+            square, square, key_grads, key_grads,
         ),
-        in_specs=[pl.BlockSpec(memory_space=pltpu.SMEM)] + [vmem] * 14,
-        out_specs=[vmem] * 10,
-        scratch_shapes=[
-            pltpu.VMEM(sums, BF16),
-            pltpu.VMEM((local_heads * tokens, HD), BF16),
-            pltpu.VMEM((local_heads * tokens, HD), BF16),
-            far, far, near, near,
-        ],
+        in_specs=[smem] + [hbm] * 12 + [smem, smem],
+        out_specs=[vmem] * 9,
+        scratch_shapes=[pltpu.VMEM(x.shape, x.dtype) for x in gdn_in + attn_in]
+        + [sems(12)]
+        + [buffer] * 4
+        + [sums(ctx, BF16), stacked, stacked, sums(ctx, F32), sums(chips, F32), sums(chips, F32)]
+        + [sums(head_devices, F32), buffer, buffer]
+        + [sems(chips)] * 4
+        + [sems(value_heads)] * 4
+        + [sems(chips)] * 4
+        + [sems(head_devices)] * 2,
         compiler_params=pltpu.CompilerParams(
             collective_id=0, has_side_effects=True, vmem_limit_bytes=VMEM_BYTES
         ),
-        name="local_part",
-    )(
-        block_lists.reshape(-1), attn_q, attn_cot, attn_lse, attn_delta, attn_k, attn_v,
-        gdn_q, gdn_k, gdn_v, gdn_cot, decay_logit, write_logit, rates, scales,
-    )
-
-    buffer = pltpu.VMEM((value_heads, GDIM, GDIM), F32)
-    sems = pltpu.SemaphoreType.DMA((value_heads,))
-    sum_sems = pltpu.SemaphoreType.DMA((ctx,))
-    head_sems = pltpu.SemaphoreType.DMA((head_devices,))
-    key_grads = jax.ShapeDtypeStruct((tokens, KV_HEADS * HD), F32)
-    mem, grad, attn_dk, attn_dv = pl.pallas_call(
-        gdn_chain,
-        out_shape=(square, square, key_grads, key_grads),
-        in_specs=[vmem] * 5,
-        out_specs=[vmem] * 4,
-        scratch_shapes=[buffer] * 4
-        + [pltpu.VMEM(sums, F32), pltpu.VMEM((head_devices, tokens, 2 * HD), F32)]
-        + [sems] * 4
-        + [sum_sems] * 2
-        + [head_sems] * 2,
-        compiler_params=pltpu.CompilerParams(
-            collective_id=1, has_side_effects=True, vmem_limit_bytes=VMEM_BYTES
-        ),
-        name="gdn_chain",
-    )(maps, maps_t, adds, pulls, dkv)
+        name="through_chain",
+    )(block_lists, *attn_in, *gdn_in, decay_rate, write_scale)
 
     dq, dk, dv, ddecay, dwrite = pl.pallas_call(
         gdn_grads,
@@ -574,14 +619,11 @@
             jax.ShapeDtypeStruct(gdn_v.shape, F32),
             gates, gates,
         ),
-        in_specs=[vmem] * 14,
+        in_specs=[vmem] * 6 + [smem, smem] + [vmem] * 6,
         out_specs=[vmem] * 5,
         compiler_params=pltpu.CompilerParams(vmem_limit_bytes=VMEM_BYTES),
         name="gdn_grads",
-    )(
-        gdn_q, gdn_k, gdn_v, gdn_cot, decay_logit, write_logit, rates, scales,
-        inverse, wu, gam, beta, mem, grad,
-    )
+    )(*gdn_in, decay_rate, write_scale, inverse, wu, gam, beta, mem, grad)
     return (grad_q, attn_dk, attn_dv, dq, dk, dv, ddecay, dwrite)
 
 

time: 104 us -> 90.4 us (0.87)
  the two profiles are of different devices: /device:TPU:25 before, /device:TPU:0 now
where the time goes in v3:
time: 90.4 us; the launch traced here: 90.1 us
  Pallas kernels  85.2 us (94%)
  local copies, waits for them, and re-layouts  4.22 us (5%)
    pallas_call x1, Pallas kernels, on_device(): pl.pallas_call(through_chain, out_shape=(jax.ShapeDtypeStruct((value_head...  76.4 us
    pallas_call x1, Pallas kernels, on_device(): pl.pallas_call(gdn_grads, out_shape=(jax.ShapeDtypeStruct(gdn_q.shape, F3...  8.82 us
    unnamed x10, local copies, waits for them, and re-layouts  4.22 us

profile of v3, /device:TPU:0, one launch (start us, length us, event | category | flops | bytes accessed | tf_op | source)
XLA Modules:
  0.0 90.1 jit_solution(7977960313185843707)
XLA Ops:
  0.6 1.4 %copy.23.lists_ref = s32[4,16,4]{2,1,0:T(8,128)} copy(s32[4,16,4]{1,2,0:T(4,128)} %param.21) | data formatting | bytes 2048 | tf_op args[6]
  2.0 76.4 %through_chain.1 = (f32[8,128,128]{2,1,0:T(8,128)}, f32[8,128,256]{2,1,0:T(8,128)}, f32[8,128]{1,0:T(8,128)}, f32[8,128]{1,0:T(8,128)}, f32[128,1024]{1,0:T(8,12...) custom-call(s32[4,16,4]{2,1,0:T(8,128)} %copy.23.lists_ref, ...), custom_call_target="tpu_custom_call" | custom-call | tf_op jit(solution)/shard_map/through_chain/pallas_call | solution.py:588
  78.4 0.0 copy-start
  78.4 8.8 %gdn_grads.1 = (f32[128,512]{1,0:T(8,128)}, f32[128,512]{1,0:T(8,128)}, f32[128,1024]{1,0:T(8,128)}, f32[8,128]{1,0:T(8,128)}, f32[8,128]{1,0:T(8,128)}) custom-call(bf16[128,512]{1,0:T(8,128)(2,1)} %q_ref.1, bf16[128,512]{1,0:T(8,128)(2,1)} %k_ref.1, bf16[128,1024]{1,0:T(8,128)(2,1)} %v_ref.1, bf16[128,1024]{1,0:T(8,128)(2,1)} %cot_ref.1, ...), custom_call_target="tpu_custom_call" | custom-call | tf_op jit(solution)/shard_map/gdn_grads/pallas_call | solution.py:614
  87.2 0.0 copy-done
  87.2 0.0 copy-start.2
  87.3 0.8 copy.27
  88.1 0.3 copy-done.2
  88.3 0.0 copy-start.1
  88.3 0.7 copy.28
  89.0 0.3 copy-done.1
  89.4 0.7 copy.29
Async XLA Ops:
  78.4 8.8 %copy-start = (f32[128,1024]{1,0:T(8,128)S(1)}, f32[128,1024]{1,0:T(8,128)}, u32[]{:S(2)}) copy-start(f32[128,1024]{1,0:T(8,128)} %get-tuple-element.44) | copy-start | bytes 1572868
  87.2 1.1 %copy-start.2 = (f32[128,512]{1,0:T(8,128)S(1)}, f32[128,512]{1,0:T(8,128)}, u32[]{:S(2)}) copy-start(f32[128,512]{1,0:T(8,128)} %get-tuple-element.45) | copy-start | bytes 786436
  88.3 1.0 %copy-start.1 = (f32[128,512]{1,0:T(8,128)S(1)}, f32[128,512]{1,0:T(8,128)}, u32[]{:S(2)}) copy-start(f32[128,512]{1,0:T(8,128)} %get-tuple-element.46) | copy-start | bytes 786436

commit v4 on v3

--- a/solution.py
+++ b/solution.py
@@ -143,7 +143,7 @@
 def gdn_grads(
     q_ref, k_ref, v_ref, cot_ref, decay_ref, write_ref, rate_ref, scale_ref,
     inv_ref, wu_ref, gam_ref, beta_ref, mem_ref, grad_ref,
-    dq_ref, dk_ref, dv_ref, ddecay_ref, dwrite_ref,
+    dq_ref, dk_ref, dv_ref, ddecay_ref, dwrite_ref, after_head,
 ):
     size = q_ref.shape[0]
     key_heads = q_ref.shape[1] // GDIM
@@ -211,6 +211,7 @@
             dbeta_rows.append(jnp.sum(by_beta.T, axis=0, keepdims=True))
             both = kept + jnp.exp(lasts[n]) * (mem[n] * grad[n])
             ends.append(jnp.sum(jnp.sum(both, axis=0, keepdims=True), axis=1, keepdims=True))
+        after_head(m)
     dlog = lane_cumsum(jnp.concatenate(dgam_rows, axis=0), True) + jnp.concatenate(ends, axis=0)
     dbeta = jnp.concatenate(dbeta_rows, axis=0)
     ddecay_ref[...] = -per_head(rate_ref, decay_ref) * sigmoid(decay_ref[...]) * dlog
@@ -249,7 +250,7 @@
             for t in range(TOPK):
                 entry = jnp.zeros((1, tokens), jnp.int32)
                 for b in range(blocks_here):
-                    listed = lists_ref[h, first + b, t]
+                    listed = lists_ref[h, t, first + b]
                     entry = jnp.where(lane // BLK == b, listed, entry)
                 hit = key_block == entry
                 member = hit if member is None else member | hit
@@ -272,7 +273,8 @@
 def through_chain(
     lists_ref, aq_hbm, acot_hbm, lse_hbm, delta_hbm, ak_hbm, av_hbm,
     q_hbm, k_hbm, v_hbm, cot_hbm, decay_hbm, write_hbm, rate_ref, scale_ref,
-    inv_ref, wu_ref, gam_ref, beta_ref, dq_ref, mem_ref, grad_ref, adk_ref, adv_ref,
+    dq_ref, adk_ref, adv_ref, gdq_ref, gdk_ref, gdv_ref, ddecay_ref, dwrite_ref,
+    inv_ref, wu_ref, gam_ref, beta_ref, mem_ref, grad_ref,
     q_ref, k_ref, v_ref, cot_ref, decay_ref, write_ref,
     aq_ref, acot_ref, lse_ref, delta_ref, ak_ref, av_ref, load_sem,
     map_ref, mapt_ref, add_ref, pull_ref, kv, q_all, cot_all, dkv, twin_in, far_in, groups,
@@ -399,13 +401,25 @@
             pair(c).wait_recv()
             dkv[2 * c + core] = dkv[2 * c + core] + twin_in[c]
 
-        @pl.when(c < chip)
-        def _():
-            down(c).start()
-
         return carry
 
     lax.fori_loop(0, chips, combine, 0)
+
+    def send_down():
+        def turn(c, carry):
+            @pl.when(c < chip)
+            def _():
+                down(c).start()
+
+            return carry
+
+        lax.fori_loop(0, chips, turn, 0)
+
+    early = 2 * chip < chips
+
+    @pl.when(early)
+    def _():
+        send_down()
 
     def share(d):
         return pltpu.make_async_remote_copy(
@@ -485,7 +499,6 @@
             copy.start()
 
     steps = 2 * value_heads
-    sum_at = jnp.minimum((chips - 1 - chip) * 5, steps - 1)
     lag = jnp.clip((n - 1 - 2 * me) * 3, -value_heads, value_heads)
     mem_late, grad_late = jnp.maximum(-lag, 0), jnp.maximum(lag, 0)
 
@@ -500,13 +513,26 @@
         def _():
             retreat(grad_head)
 
-        @pl.when(step == sum_at)
+        @pl.when((step == value_heads - 1) & jnp.logical_not(early))
+        def _():
+            send_down()
+
+        return carry
+
+    lax.fori_loop(0, steps, turn, 0)
+
+    def after_head(m):
+        @pl.when(sum_slot == m + 1)
         def _():
             finish_sum()
 
-        return carry
-
-    lax.fori_loop(0, steps, turn, 0)
+    sum_slot = jnp.minimum(chips - 1 - chip, q_ref.shape[1] // GDIM)
+    after_head(-1)
+    gdn_grads(
+        q_ref, k_ref, v_ref, cot_ref, decay_ref, write_ref, rate_ref, scale_ref,
+        inv_ref, wu_ref, gam_ref, beta_ref, mem_ref, grad_ref,
+        gdq_ref, gdk_ref, gdv_ref, ddecay_ref, dwrite_ref, after_head,
+    )
 
     def drain(head, carry):
         @pl.when(me < n - 1)
@@ -558,6 +584,17 @@
         copy(source(d), near_send, near_recv, d, twin).wait_send()
 
 
+def hand_over(*refs):
+    count = len(refs) // 2
+    copies = [
+        pltpu.make_async_copy(refs[i], refs[count + i], refs[-1].at[i]) for i in range(count)
+    ]
+    for copy in copies:
+        copy.start()
+    for copy in copies:
+        copy.wait()
+
+
 def on_device(
     attn_q, attn_k, attn_v, attn_cot, attn_lse, attn_delta, block_lists,
     gdn_q, gdn_k, gdn_v, decay_logit, write_logit, decay_rate, write_scale, gdn_cot,
@@ -569,7 +606,6 @@
     value_heads = gdn_v.shape[1] // GDIM
     vmem, smem = (pl.BlockSpec(memory_space=space) for space in (pltpu.VMEM, pltpu.SMEM))
 
-    square = jax.ShapeDtypeStruct((value_heads, GDIM, GDIM), F32)
     gates = jax.ShapeDtypeStruct((value_heads, tokens), F32)
     key_grads = jax.ShapeDtypeStruct((tokens, KV_HEADS * HD), F32)
     buffer = pltpu.VMEM((value_heads, GDIM, GDIM), F32)
@@ -585,18 +621,25 @@
     gdn_in = (gdn_q, gdn_k, gdn_v, gdn_cot, decay_logit, write_logit)
     chips = ctx // 2
     hbm = pl.BlockSpec(memory_space=pltpu.HBM)
-    inverse, wu, gam, beta, grad_q, mem, grad, attn_dk, attn_dv = pl.pallas_call(
+    results = (
+        jax.ShapeDtypeStruct(attn_q.shape, F32),
+        key_grads, key_grads,
+        *(jax.ShapeDtypeStruct(x.shape, F32) for x in (gdn_q, gdn_k, gdn_v)),
+        gates, gates,
+    )
+    held = pl.pallas_call(
         through_chain,
-        out_shape=(
-            jax.ShapeDtypeStruct((value_heads, tokens, tokens), F32),
-            jax.ShapeDtypeStruct((value_heads, tokens, 2 * GDIM), F32),
-            gates, gates,
-            jax.ShapeDtypeStruct((tokens, local_heads * HD), F32),
-            square, square, key_grads, key_grads,
-        ),
+        out_shape=results,
         in_specs=[smem] + [hbm] * 12 + [smem, smem],
-        out_specs=[vmem] * 9,
-        scratch_shapes=[pltpu.VMEM(x.shape, x.dtype) for x in gdn_in + attn_in]
+        out_specs=[vmem] * 8,
+        scratch_shapes=[
+            pltpu.VMEM((value_heads, tokens, tokens), F32),
+            pltpu.VMEM((value_heads, tokens, 2 * GDIM), F32),
+            pltpu.VMEM(gates.shape, F32),
+            pltpu.VMEM(gates.shape, F32),
+            buffer, buffer,
+        ]
+        + [pltpu.VMEM(x.shape, x.dtype) for x in gdn_in + attn_in]
         + [sems(12)]
         + [buffer] * 4
         + [sums(ctx, BF16), stacked, stacked, sums(ctx, F32), sums(chips, F32), sums(chips, F32)]
@@ -609,22 +652,17 @@
             collective_id=0, has_side_effects=True, vmem_limit_bytes=VMEM_BYTES
         ),
         name="through_chain",
-    )(block_lists, *attn_in, *gdn_in, decay_rate, write_scale)
-
-    dq, dk, dv, ddecay, dwrite = pl.pallas_call(
-        gdn_grads,
-        out_shape=(
-            jax.ShapeDtypeStruct(gdn_q.shape, F32),
-            jax.ShapeDtypeStruct(gdn_k.shape, F32),
-            jax.ShapeDtypeStruct(gdn_v.shape, F32),
-            gates, gates,
-        ),
-        in_specs=[vmem] * 6 + [smem, smem] + [vmem] * 6,
-        out_specs=[vmem] * 5,
+    )(block_lists.transpose(0, 2, 1), *attn_in, *gdn_in, decay_rate, write_scale)
+
+    return pl.pallas_call(
+        hand_over,
+        out_shape=results,
+        in_specs=[hbm] * len(results),
+        out_specs=[hbm] * len(results),
+        scratch_shapes=[sems(len(results))],
         compiler_params=pltpu.CompilerParams(vmem_limit_bytes=VMEM_BYTES),
-        name="gdn_grads",
-    )(*gdn_in, decay_rate, write_scale, inverse, wu, gam, beta, mem, grad)
-    return (grad_q, attn_dk, attn_dv, dq, dk, dv, ddecay, dwrite)
+        name="hand_over",
+    )(*held)
 
 
 def solution(mesh):

time: 90.4 us -> 143 us (1.58)
  Pallas kernels: 85.2 us -> 142 us
  local copies, waits for them, and re-layouts: 4.22 us -> 0 us
    pallas_call x2, Pallas kernels: 85.2 us -> 142 us  [the longest x1 77.4 us: on_device(): pl.pallas_call(through_chain, out_shape=results, in_specs=[smem] + [hbm]...]
    unnamed x10 -> x0, local copies, waits for them, and re-layouts: 4.22 us -> none
where the time goes in v4:
time: 143 us
  Pallas kernels  142 us (99%)
    pallas_call x1, Pallas kernels, on_device(): pl.pallas_call(through_chain, out_shape=results, in_specs=[smem] + [hbm]...  77.4 us
    pallas_call x1, Pallas kernels, on_device(): pl.pallas_call(hand_over, out_shape=results, in_specs=[hbm] * len(results...  65 us

profile of v4, /device:TPU:0, one launch (start us, length us, event | category | flops | bytes accessed | tf_op | source)
XLA Modules:
  0.0 143.2 jit_solution(1663561725525298959)
XLA Ops:
  0.6 77.4 %through_chain.1 = (f32[128,1024]{1,0:T(8,128)}, f32[128,512]{1,0:T(8,128)}, f32[128,512]{1,0:T(8,128)}, f32[128,512]{1,0:T(8,128)}, f32[128,512]{1,0:T(8,128)},...) custom-call(s32[4,4,16]{2,1,0:T(4,128)} %bitcast.1, bf16[128,1024]{1,0:T(8,128)(2,1)} %aq_hbm.1, ...), custom_call_target="tpu_custom_call" | custom-call | tf_op jit(solution)/shard_map/through_chain/pallas_call | solution.py:630
  78.0 65.0 %hand_over.1 = (f32[128,1024]{1,0:T(8,128)}, f32[128,512]{1,0:T(8,128)}, f32[128,512]{1,0:T(8,128)}, f32[128,512]{1,0:T(8,128)}, f32[128,512]{1,0:T(8,128)}, /*i...) custom-call(f32[128,1024]{1,0:T(8,128)} %get-tuple-element.16.refs_0_, ...), custom_call_target="tpu_custom_call" | custom-call | tf_op jit(solution)/shard_map/hand_over/pallas_call | solution.py:657

commit v5 on v4

--- a/solution.py
+++ b/solution.py
@@ -586,13 +586,8 @@
 
 def hand_over(*refs):
     count = len(refs) // 2
-    copies = [
-        pltpu.make_async_copy(refs[i], refs[count + i], refs[-1].at[i]) for i in range(count)
-    ]
-    for copy in copies:
-        copy.start()
-    for copy in copies:
-        copy.wait()
+    for i in range(count):
+        refs[count + i][...] = refs[i][...]
 
 
 def on_device(
@@ -657,9 +652,8 @@
     return pl.pallas_call(
         hand_over,
         out_shape=results,
-        in_specs=[hbm] * len(results),
-        out_specs=[hbm] * len(results),
-        scratch_shapes=[sems(len(results))],
+        in_specs=[vmem] * len(results),
+        out_specs=[vmem] * len(results),
         compiler_params=pltpu.CompilerParams(vmem_limit_bytes=VMEM_BYTES),
         name="hand_over",
     )(*held)

time: 143 us -> 81.2 us (0.57)
  Pallas kernels: 142 us -> 80.2 us
    pallas_call x1, Pallas kernels: 65 us -> 2.84 us  [on_device(): pl.pallas_call(hand_over, out_shape=results, in_specs=[vmem] * len(result...]
where the time goes in v5:
time: 81.2 us; the launch traced here: 80.9 us
  Pallas kernels  80.2 us (99%)
    pallas_call x1, Pallas kernels, on_device(): pl.pallas_call(through_chain, out_shape=results, in_specs=[smem] + [hbm]...  77.4 us
    pallas_call x1, Pallas kernels, on_device(): pl.pallas_call(hand_over, out_shape=results, in_specs=[vmem] * len(result...  2.84 us

profile of v5, /device:TPU:0, one launch (start us, length us, event | category | flops | bytes accessed | tf_op | source)
XLA Modules:
  0.0 80.9 jit_solution(18121036803829512814)
XLA Ops:
  0.6 77.4 %through_chain.1 = (f32[128,1024]{1,0:T(8,128)}, f32[128,512]{1,0:T(8,128)}, f32[128,512]{1,0:T(8,128)}, f32[128,512]{1,0:T(8,128)}, f32[128,512]{1,0:T(8,128)},...) custom-call(s32[4,4,16]{2,1,0:T(4,128)} %bitcast.1, bf16[128,1024]{1,0:T(8,128)(2,1)} %aq_hbm.1, ...), custom_call_target="tpu_custom_call" | custom-call | tf_op jit(solution)/shard_map/through_chain/pallas_call | solution.py:625
  78.0 2.8 %hand_over.1 = (f32[128,1024]{1,0:T(8,128)}, f32[128,512]{1,0:T(8,128)}, f32[128,512]{1,0:T(8,128)}, f32[128,512]{1,0:T(8,128)}, f32[128,512]{1,0:T(8,128)}, /*i...) custom-call(f32[128,1024]{1,0:T(8,128)} %get-tuple-element.16.refs_0_, ...), custom_call_target="tpu_custom_call" | custom-call | tf_op jit(solution)/shard_map/hand_over/pallas_call | solution.py:652
